TPU v7x, 32 devices: a whole 2x2x4 slice. The times are simulated.
32 devices in a mesh: shot: 8 (over z, y), rcv: 4 (over x, core).
Axes of the slice: x: 2, y: 2, z: 4, core: 2. Of those that a mesh axis runs over, the one named last changes fastest.
Arguments:
- record: bfloat16 [8192, 2048], P('shot', 'rcv'), may hold values from -6 to 6
- offsets: int32 [8], P('shot'), may hold values from 0 to 1023
- lengths: int32 [8], P('shot'), may hold values from 1024 to 2048
- thresholds: float32 [3], replicated, may hold values from 0.05 to 0.5
Outputs:
- estimate: float32 [8, 2048, 2048], P('shot', None, 'rcv')
All inputs are finite; a program needn't handle non-finite values.
Results may differ from a plain program's by a relative error of at most 0.0003.
Values sent between devices are 32-bit elements; how exact they have to be, the bound alone decides.
No kernel may reach another device: no remote copies, remote signals or barrier semaphores. Data moves between devices by JAX's collectives and lax.ppermute only.
A program may use at most 64 MiB of HBM per device.

v0:
```python
import jax
import jax.numpy as jnp
from jax import lax
from jax.sharding import PartitionSpec as P

LEVELS = 3
ITERS = 2


SPLINE_TAPS = (0.0625, 0.25, 0.375, 0.25, 0.0625)
relax_step = 0.5


def with_halo(cells, sides, width):
    for axis, dim in sides:
        count = lax.axis_size(axis)
        ends = count - 1
        head = lax.slice_in_dim(cells, 0, width, axis=dim)
        tail = lax.slice_in_dim(cells, cells.shape[dim] - width, cells.shape[dim], axis=dim)
        cells = jnp.concatenate(
            [
                lax.ppermute(tail, axis, [(i, (i + 1) % count) for i in range(ends)]),
                cells,
                lax.ppermute(head, axis, [((i + 1) % count, i) for i in range(ends)]),
            ],
            axis=dim,
        )
    return cells


def shifted(shard, axis, by):
    devices = lax.axis_size(axis)
    pairs = [(i, i + by) for i in range(devices) if 0 <= i + by < devices]
    return lax.ppermute(shard, axis, pairs)


def smooth_time(signal, dilation):
    length_rows = signal.shape[0]
    padded = jnp.pad(signal, ((2 * dilation, 2 * dilation), (0, 0)))
    summed = SPLINE_TAPS[0] * padded[0:length_rows]
    for tap_index in range(1, 5):
        summed = (
            summed
            + SPLINE_TAPS[tap_index]
            * padded[tap_index * dilation : tap_index * dilation + length_rows]
        )
    return summed


def filter_columns(extended, dilation, narrow):
    summed = SPLINE_TAPS[0] * extended[:, 0:narrow]
    for tap_index in range(1, 5):
        summed = (
            summed
            + SPLINE_TAPS[tap_index]
            * extended[:, tap_index * dilation : tap_index * dilation + narrow]
        )
    return summed


def soft_limit(values, level_cut):
    return values - jnp.clip(values, -level_cut, level_cut)


def shrink_each(signal, thresholds):
    columns = signal.shape[1]
    current = signal
    shrunk = jnp.zeros_like(signal)
    for level_index in range(LEVELS):
        dilation = 2**level_index
        smoothed = smooth_time(current, dilation)
        extended = with_halo(smoothed, (("rcv", 1),), 2 * dilation)
        coarser = filter_columns(extended, dilation, columns)
        shrunk = shrunk + soft_limit(current - coarser, thresholds[level_index])
        current = coarser
    return shrunk + current


def on_device(record, offsets, lengths, thresholds):
    seg_len = record.shape[0]
    columns = record.shape[1]
    window = 2 * seg_len
    anchor = offsets[0]
    live_mask = (lax.broadcasted_iota(jnp.int32, (window, 1), 0) < lengths[0]).astype(jnp.float32)
    measured = record.astype(jnp.float32)
    estimate = jnp.zeros((window, columns), jnp.float32)
    for sweep_index in range(ITERS):
        if sweep_index == 0:
            misfit = measured
        else:
            placed = lax.dynamic_update_slice(
                jnp.zeros((3 * seg_len, columns), jnp.float32), estimate, (anchor, jnp.int32(0))
            )
            own_part = placed[:seg_len]
            near_part = placed[seg_len : 2 * seg_len]
            far_part = placed[2 * seg_len :]
            arrived = shifted(near_part, "shot", 1) + shifted(far_part, "shot", 2)
            misfit = measured - (own_part + arrived)
        following = shifted(misfit, "shot", -1)
        second = shifted(misfit, "shot", -2)
        extended = jnp.concatenate([misfit, following, second], axis=0)
        windowed = lax.dynamic_slice(extended, (anchor, jnp.int32(0)), (window, columns))
        gathered = estimate + relax_step * live_mask * windowed
        estimate = live_mask * shrink_each(gathered, thresholds)
    return estimate[None]


def solution(mesh):
    return jax.shard_map(
        on_device,
        mesh=mesh,
        in_specs=(P("shot", "rcv"), P("shot"), P("shot"), P()),
        out_specs=P("shot", None, "rcv"),
        check_vma=False,
    )
```

profile of v0, /device:TPU:9, one launch (start us, length us, event | category | flops | bytes accessed | tf_op | source)
XLA Modules:
  0.0 437.6 jit_solution(12764606559874927015)
XLA Ops:
  3.1 3.0 collective-permute-start
  9.3 42.4 %collective-permute-done = f32[1024,512]{0,1:T(8,128)} collective-permute-done((f32[1024,512]{0,1:T(8,128)}, f32[1024,512]{0,1:T(8,128)}, u32[]{:S(2)}, u32[]{:S(2)}) %collective-permute-start) | collective-permute-done | bytes 2097184 | tf_op jit(solution)/shard_map/ppermute | solution.py:34
  51.8 45.9 %collective-permute-done.1 = f32[1024,512]{0,1:T(8,128)} collective-permute-done((f32[1024,512]{0,1:T(8,128)}, f32[1024,512]{0,1:T(8,128)}, u32[]{:S(2)}, u32[]{:S(2)}) %collective-permute-start.1) | collective-permute-done | bytes 2097184 | tf_op jit(solution)/shard_map/ppermute | solution.py:34
  97.7 5.0 %fusion.54 = f32[2048,512]{0,1:T(8,128)S(1)} fusion(s32[]{:T(128)S(6)} %select_n.2, f32[1024,512]{0,1:T(8,128)} %convert_element_type.21, f32[1024,512]{0,1:T(8,128)} %collective-permute-done, f32[1024,512]{0,1:T(8,128)} %collective-permute-done.1, f32[2048]{0:T(1024)S(1)} %fusion.74), kind=kLoop, calls=%fused_computation.84 | loop fusion | flops 3145728 | bytes 10493956 | tf_op jit(solution)/shard_map/mul | solution.py:103
  102.7 4.9 %multiply_add_fusion.5 = f32[2048,512]{0,1:T(8,128)S(1)} fusion(f32[2048,512]{0,1:T(8,128)S(1)} %fusion.54), kind=kLoop, calls=%fused_computation.126 | loop fusion | flops 9437184 | bytes 8388608 | tf_op jit(solution)/shard_map/add | solution.py:43
  107.6 4.6 %collective-permute-start.2 = (f32[2048,2]{0,1:T(2,128)S(1)}, f32[2048,2]{0,1:T(2,128)S(1)}, u32[]{:S(2)}, u32[]{:S(2)}) collective-permute-start(f32[2048,2]{0,1:T(2,128)S(1)} %get-tuple-element.17), channel_id=1, source_target_pairs={{0,1},{1,2},{2,3},{4,5},{5,6},{6,7},{8,9},{9,10},{10,11},{12,13},{... | collective-permute-start | bytes 49160 | tf_op jit(solution)/shard_map/ppermute | solution.py:22
  114.1 3.1 collective-permute-done.3
  117.2 2.7 fusion.43
  119.9 4.9 %multiply_add_fusion.4 = f32[2048,512]{0,1:T(8,128)S(1)} fusion(f32[2048,512]{0,1:T(8,128)S(1)} %fusion.43), kind=kLoop, calls=%fused_computation.123 | loop fusion | flops 9437184 | bytes 8388608 | tf_op jit(solution)/shard_map/add | solution.py:43
  128.8 2.6 collective-permute-start.5
  134.0 9.0 %fusion.35 = f32[2048,512]{0,1:T(8,128)S(1)} fusion(f32[2048,512]{0,1:T(8,128)} %copy-done.5, f32[2048,4]{0,1:T(4,128)S(1)} %collective-permute-done.5, f32[2048,4]{0,1:T(4,128)S(1)} %collective-permute-done.4), kind=kLoop, calls=%fused_computation.65 | loop fusion | flops 13631488 | bytes 8454144 | tf_op jit(solution)/shard_map/add | solution.py:54
  143.0 4.9 %multiply_add_fusion.3 = f32[2048,512]{0,1:T(8,128)S(1)} fusion(f32[2048,512]{0,1:T(8,128)S(1)} %fusion.35), kind=kLoop, calls=%fused_computation.120 | loop fusion | flops 9437184 | bytes 8388608 | tf_op jit(solution)/shard_map/add | solution.py:43
  148.0 3.0 collective-permute-start.6
  152.9 3.6 collective-permute-done.7
  156.6 7.0 %add_multiply_fusion = f32[2048,512]{0,1:T(8,128)} fusion(f32[2048,512]{0,1:T(8,128)S(1)} %fusion.35, f32[2048,8]{0,1:T(8,128)S(1)} %collective-permute-done.7, f32[2048,512]{0,1:T(8,128)S(1)} %multiply_add_fusion.3, f32[2048,8]{0,1:T(8,128)S(1)} %collective-permute-done.6, f32[2048,512]{0,1:T(8,128)S(1)} %copy-done.3, f32[2048,512]{0,1:T(8,128)S(1)} %copy-done.1, ...), kind=kLoop, calls=%fused_computation.119 | loop fusion | flops 30408704 | bytes 21110808 | tf_op jit(solution)/shard_map/mul | solution.py:104
  163.5 3.4 broadcast_in_dim.6
  166.9 22.2 %dynamic_update_slice.3 = f32[3072,512]{0,1:T(8,128)} dynamic-update-slice(f32[3072,512]{0,1:T(8,128)} %broadcast_in_dim.6, f32[2048,512]{0,1:T(8,128)} %add_multiply_fusion, s32[]{:T(128)S(6)} %select_n.2, s32[]{:T(128)} %constant.4.clone.1) | dynamic-update-slice | bytes 8388612 | tf_op jit(solution)/shard_map/dynamic_update_slice | solution.py:91
  195.8 46.1 %collective-permute-done.8 = f32[1024,512]{0,1:T(8,128)S(1)} collective-permute-done((f32[1024,512]{0,1:T(8,128)S(1)}, f32[1024,512]{0,1:T(8,128)S(1)}, u32[]{:S(2)}, u32[]{:S(2)}) %collective-permute-start.8) | collective-permute-done | bytes 2097184 | tf_op jit(solution)/shard_map/ppermute | solution.py:34
  244.3 44.4 %collective-permute-start.10 = (f32[1024,512]{0,1:T(8,128)S(1)}, f32[1024,512]{0,1:T(8,128)S(1)}, u32[]{:S(2)}, u32[]{:S(2)}) collective-permute-start(f32[1024,512]{0,1:T(8,128)S(1)} %fusion.73), channel_id=1, source_target_pairs={{4,0},{8,4},{12,8},{16,12},{20,16},{24,20},{28,24},{5,1},{9,5},{13... | collective-permute-start | bytes 6291464 | tf_op jit(solution)/shard_map/ppermute | solution.py:34
  290.9 43.3 %collective-permute-done.10 = f32[1024,512]{0,1:T(8,128)S(1)} collective-permute-done((f32[1024,512]{0,1:T(8,128)S(1)}, f32[1024,512]{0,1:T(8,128)S(1)}, u32[]{:S(2)}, u32[]{:S(2)}) %collective-permute-start.10) | collective-permute-done | bytes 2097184 | tf_op jit(solution)/shard_map/ppermute | solution.py:34
  334.2 46.4 %collective-permute-done.11 = f32[1024,512]{0,1:T(8,128)S(1)} collective-permute-done((f32[1024,512]{0,1:T(8,128)S(1)}, f32[1024,512]{0,1:T(8,128)S(1)}, u32[]{:S(2)}, u32[]{:S(2)}) %collective-permute-start.11) | collective-permute-done | bytes 2097184 | tf_op jit(solution)/shard_map/ppermute | solution.py:34
  380.6 2.9 fusion.51
  383.4 4.9 %multiply_add_fusion.2 = f32[2048,512]{0,1:T(8,128)S(1)} fusion(f32[2048,512]{0,1:T(8,128)S(1)} %fusion.51), kind=kLoop, calls=%fused_computation.116 | loop fusion | flops 9437184 | bytes 8388608 | tf_op jit(solution)/shard_map/add | solution.py:43
  392.7 2.6 collective-permute-done.13
  395.3 2.7 fusion.19
  398.0 4.9 %multiply_add_fusion.1 = f32[2048,512]{0,1:T(8,128)S(1)} fusion(f32[2048,512]{0,1:T(8,128)S(1)} %fusion.19), kind=kLoop, calls=%fused_computation.113 | loop fusion | flops 9437184 | bytes 8388608 | tf_op jit(solution)/shard_map/add | solution.py:43
  407.3 2.8 collective-permute-done.15
  410.1 2.7 fusion.11
  412.8 4.9 %multiply_add_fusion = f32[2048,512]{0,1:T(8,128)S(1)} fusion(f32[2048,512]{0,1:T(8,128)S(1)} %fusion.11), kind=kLoop, calls=%fused_computation.110 | loop fusion | flops 9437184 | bytes 8388608 | tf_op jit(solution)/shard_map/add | solution.py:43
  422.0 3.2 collective-permute-done.17
  425.2 7.1 %multiply_bitcast_fusion = f32[1,2048,512]{1,2,0:T(8,128)} fusion(f32[2048,512]{0,1:T(8,128)S(1)} %fusion.11, f32[2048,8]{0,1:T(8,128)S(1)} %collective-permute-done.17, f32[2048,512]{0,1:T(8,128)S(1)} %multiply_add_fusion, f32[2048,8]{0,1:T(8,128)S(1)} %collective-permute-done.16, f32[2048,512]{0,1:T(8,128)S(1)} %fusion.19, f32[2048,512]{0,1:T(8,128)S(1)} %fusion.51, ...), kind=kLoop, calls=%fused_computation.109 | loop fusion | flops 30408704 | bytes 21110808 | tf_op jit(solution)/shard_map/broadcast_in_dim | solution.py:105
  432.3 5.3 %copy.6 = f32[1,2048,512]{2,1,0:T(8,128)} copy(f32[1,2048,512]{1,2,0:T(8,128)} %multiply_bitcast_fusion) | data formatting | bytes 8388608 | tf_op jit(solution)/shard_map/broadcast_in_dim | solution.py:105
  (48 shorter events, 37.9 us)
Async XLA Ops:
  3.1 48.7 %collective-permute-start = (f32[1024,512]{0,1:T(8,128)}, f32[1024,512]{0,1:T(8,128)}, u32[]{:S(2)}, u32[]{:S(2)}) collective-permute-start(f32[1024,512]{0,1:T(8,128)} %convert_element_type.21), channel_id=1, source_target_pairs={{4,0},{8,4},{12,8},{16,12},{20,16},{24,20},{28,24},{5,1},{9,5},{13... | collective-permute-start | bytes 6291464 | tf_op jit(solution)/shard_map/ppermute | solution.py:34
  6.1 91.6 %collective-permute-start.1 = (f32[1024,512]{0,1:T(8,128)}, f32[1024,512]{0,1:T(8,128)}, u32[]{:S(2)}, u32[]{:S(2)}) collective-permute-start(f32[1024,512]{0,1:T(8,128)} %convert_element_type.21), channel_id=1, source_target_pairs={{8,0},{12,4},{16,8},{20,12},{24,16},{28,20},{9,1},{13,5},{17,9},{2... | collective-permute-start | bytes 6291464 | tf_op jit(solution)/shard_map/ppermute | solution.py:34
  102.7 4.9 %copy-start = (f32[2048,512]{0,1:T(8,128)}, f32[2048,512]{0,1:T(8,128)S(1)}, u32[]{:S(2)}) copy-start(f32[2048,512]{0,1:T(8,128)S(1)} %fusion.54) | copy-start | bytes 12582916
  107.6 6.5 %collective-permute-start.2 = (f32[2048,2]{0,1:T(2,128)S(1)}, f32[2048,2]{0,1:T(2,128)S(1)}, u32[]{:S(2)}, u32[]{:S(2)}) collective-permute-start(f32[2048,2]{0,1:T(2,128)S(1)} %get-tuple-element.17), channel_id=1, source_target_pairs={{0,1},{1,2},{2,3},{4,5},{5,6},{6,7},{8,9},{9,10},{10,11},{12,13},{... | collective-permute-start | bytes 49160 | tf_op jit(solution)/shard_map/ppermute | solution.py:22
  112.2 5.1 %collective-permute-start.3 = (f32[2048,2]{0,1:T(2,128)S(1)}, f32[2048,2]{0,1:T(2,128)S(1)}, u32[]{:S(2)}, u32[]{:S(2)}) collective-permute-start(f32[2048,2]{0,1:T(2,128)S(1)} %get-tuple-element.18), channel_id=1, source_target_pairs={{1,0},{2,1},{3,2},{5,4},{6,5},{7,6},{9,8},{10,9},{11,10},{13,12},{... | collective-permute-start | bytes 49160 | tf_op jit(solution)/shard_map/ppermute | solution.py:24
  119.9 5.0 %copy-start.2 = (f32[2048,512]{0,1:T(8,128)}, f32[2048,512]{0,1:T(8,128)S(1)}, u32[]{:S(2)}) copy-start(f32[2048,512]{0,1:T(8,128)S(1)} %fusion.43) | copy-start | bytes 12582916
  119.9 11.4 %copy-start.6 = (f32[3]{0:T(128)S(1)}, f32[3]{0:T(128)}, u32[]{:S(2)}) copy-start(f32[3]{0:T(128)} %param.7) | copy-start | bytes 40
  124.8 2.0 copy-start.5
  126.8 7.0 %collective-permute-start.4 = (f32[2048,4]{0,1:T(4,128)S(1)}, f32[2048,4]{0,1:T(4,128)S(1)}, u32[]{:S(2)}, u32[]{:S(2)}) collective-permute-start(f32[2048,4]{0,1:T(4,128)S(1)} %get-tuple-element.15), channel_id=1, source_target_pairs={{0,1},{1,2},{2,3},{4,5},{5,6},{6,7},{8,9},{9,10},{10,11},{12,13},{... | collective-permute-start | bytes 98312 | tf_op jit(solution)/shard_map/ppermute | solution.py:22
  128.8 5.2 %collective-permute-start.5 = (f32[2048,4]{0,1:T(4,128)S(1)}, f32[2048,4]{0,1:T(4,128)S(1)}, u32[]{:S(2)}, u32[]{:S(2)}) collective-permute-start(f32[2048,4]{0,1:T(4,128)S(1)} %get-tuple-element.16), channel_id=1, source_target_pairs={{1,0},{2,1},{3,2},{5,4},{6,5},{7,6},{9,8},{10,9},{11,10},{13,12},{... | collective-permute-start | bytes 98312 | tf_op jit(solution)/shard_map/ppermute | solution.py:24
  143.0 13.5 %copy-start.1 = (f32[2048,512]{0,1:T(8,128)S(1)}, f32[2048,512]{0,1:T(8,128)}, u32[]{:S(2)}) copy-start(f32[2048,512]{0,1:T(8,128)} %copy-done) | copy-start | bytes 12582916
  143.0 13.5 %copy-start.3 = (f32[2048,512]{0,1:T(8,128)S(1)}, f32[2048,512]{0,1:T(8,128)}, u32[]{:S(2)}) copy-start(f32[2048,512]{0,1:T(8,128)} %copy-done.2) | copy-start | bytes 12582916
  148.0 5.0 %collective-permute-start.6 = (f32[2048,8]{0,1:T(8,128)S(1)}, f32[2048,8]{0,1:T(8,128)S(1)}, u32[]{:S(2)}, u32[]{:S(2)}) collective-permute-start(f32[2048,8]{0,1:T(8,128)S(1)} %get-tuple-element.13), channel_id=1, source_target_pairs={{0,1},{1,2},{2,3},{4,5},{5,6},{6,7},{8,9},{9,10},{10,11},{12,13},{... | collective-permute-start | bytes 196616 | tf_op jit(solution)/shard_map/ppermute | solution.py:22
  151.0 5.6 %collective-permute-start.7 = (f32[2048,8]{0,1:T(8,128)S(1)}, f32[2048,8]{0,1:T(8,128)S(1)}, u32[]{:S(2)}, u32[]{:S(2)}) collective-permute-start(f32[2048,8]{0,1:T(8,128)S(1)} %get-tuple-element.14), channel_id=1, source_target_pairs={{1,0},{2,1},{3,2},{5,4},{6,5},{7,6},{9,8},{10,9},{11,10},{13,12},{... | collective-permute-start | bytes 196616 | tf_op jit(solution)/shard_map/ppermute | solution.py:24
  191.7 50.2 %collective-permute-start.8 = (f32[1024,512]{0,1:T(8,128)S(1)}, f32[1024,512]{0,1:T(8,128)S(1)}, u32[]{:S(2)}, u32[]{:S(2)}) collective-permute-start(f32[1024,512]{0,1:T(8,128)S(1)} %get-tuple-element.6), channel_id=1, source_target_pairs={{0,4},{4,8},{8,12},{12,16},{16,20},{20,24},{24,28},{1,5},{5,9},{9,... | collective-permute-start | bytes 6291464 | tf_op jit(solution)/shard_map/ppermute | solution.py:34
  193.6 187.0 %copy-start.4 = (f32[2048,512]{0,1:T(8,128)S(1)}, f32[2048,512]{0,1:T(8,128)}, u32[]{:S(2)}) copy-start(f32[2048,512]{0,1:T(8,128)} %add_multiply_fusion) | copy-start | bytes 12582916
  193.6 48.3 %collective-permute-start.9 = (f32[1024,512]{0,1:T(8,128)S(1)}, f32[1024,512]{0,1:T(8,128)S(1)}, u32[]{:S(2)}, u32[]{:S(2)}) collective-permute-start(f32[1024,512]{0,1:T(8,128)S(1)} %get-tuple-element.5), channel_id=1, source_target_pairs={{0,8},{4,12},{8,16},{12,20},{16,24},{20,28},{1,9},{5,13},{9,17},{1... | collective-permute-start | bytes 6291464 | tf_op jit(solution)/shard_map/ppermute | solution.py:34
  244.3 89.8 %collective-permute-start.10 = (f32[1024,512]{0,1:T(8,128)S(1)}, f32[1024,512]{0,1:T(8,128)S(1)}, u32[]{:S(2)}, u32[]{:S(2)}) collective-permute-start(f32[1024,512]{0,1:T(8,128)S(1)} %fusion.73), channel_id=1, source_target_pairs={{4,0},{8,4},{12,8},{16,12},{20,16},{24,20},{28,24},{5,1},{9,5},{13... | collective-permute-start | bytes 6291464 | tf_op jit(solution)/shard_map/ppermute | solution.py:34
  288.7 91.8 %collective-permute-start.11 = (f32[1024,512]{0,1:T(8,128)S(1)}, f32[1024,512]{0,1:T(8,128)S(1)}, u32[]{:S(2)}, u32[]{:S(2)}) collective-permute-start(f32[1024,512]{0,1:T(8,128)S(1)} %fusion.73), channel_id=1, source_target_pairs={{8,0},{12,4},{16,8},{20,12},{24,16},{28,20},{9,1},{13,5},{17,9},{2... | collective-permute-start | bytes 6291464 | tf_op jit(solution)/shard_map/ppermute | solution.py:34
  388.4 4.3 collective-permute-start.12
  390.3 5.1 %collective-permute-start.13 = (f32[2048,2]{0,1:T(2,128)S(1)}, f32[2048,2]{0,1:T(2,128)S(1)}, u32[]{:S(2)}, u32[]{:S(2)}) collective-permute-start(f32[2048,2]{0,1:T(2,128)S(1)} %get-tuple-element.12), channel_id=1, source_target_pairs={{1,0},{2,1},{3,2},{5,4},{6,5},{7,6},{9,8},{10,9},{11,10},{13,12},{... | collective-permute-start | bytes 49160 | tf_op jit(solution)/shard_map/ppermute | solution.py:24
  402.9 4.3 collective-permute-start.14
  404.9 5.2 %collective-permute-start.15 = (f32[2048,4]{0,1:T(4,128)S(1)}, f32[2048,4]{0,1:T(4,128)S(1)}, u32[]{:S(2)}, u32[]{:S(2)}) collective-permute-start(f32[2048,4]{0,1:T(4,128)S(1)} %get-tuple-element.10), channel_id=1, source_target_pairs={{1,0},{2,1},{3,2},{5,4},{6,5},{7,6},{9,8},{10,9},{11,10},{13,12},{... | collective-permute-start | bytes 98312 | tf_op jit(solution)/shard_map/ppermute | solution.py:24
  417.7 4.3 collective-permute-start.16
  419.6 5.6 %collective-permute-start.17 = (f32[2048,8]{0,1:T(8,128)S(1)}, f32[2048,8]{0,1:T(8,128)S(1)}, u32[]{:S(2)}, u32[]{:S(2)}) collective-permute-start(f32[2048,8]{0,1:T(8,128)S(1)} %get-tuple-element.8), channel_id=1, source_target_pairs={{1,0},{2,1},{3,2},{5,4},{6,5},{7,6},{9,8},{10,9},{11,10},{13,12},{... | collective-permute-start | bytes 196616 | tf_op jit(solution)/shard_map/ppermute | solution.py:24
where the time goes:
time: 439 us; the launch traced here: 438 us
  waiting for transfers between devices  240 us (55%)
  starting transfers between devices  84.4 us (19%)
  other arithmetic  72.3 us (16%)
  local copies, waits for them, and re-layouts  37.7 us (9%)
    ppermute x6, waiting for transfers between devices, shifted(): return lax.ppermute(shard, axis, pairs)  224 us
    ppermute x6, starting transfers between devices, shifted(): return lax.ppermute(shard, axis, pairs)  55.6 us
    add x6, other arithmetic, smooth_time(): summed + SPLINE_TAPS[tap_index] * padded[tap_index * dilation:tap_index *...  29.4 us
    dynamic_update_slice x1, local copies, waits for them, and re-layouts, on_device(): lax.dynamic_update_slice(jnp.zeros((3 * seg_len, columns), jnp.float32),...  22.2 us
    add x4, other arithmetic, filter_columns(): summed + SPLINE_TAPS[tap_index] * extended[:, tap_index * dilation:tap_in...  16.9 us
    ppermute x6, waiting for transfers between devices, with_halo(): lax.ppermute(head, axis, [((i + 1) % count, i) for i in range(ends)])  15.6 us
    ppermute x6, starting transfers between devices, with_halo(): lax.ppermute(tail, axis, [(i, (i + 1) % count) for i in range(ends)])  15.3 us
    ppermute x6, starting transfers between devices, with_halo(): lax.ppermute(head, axis, [((i + 1) % count, i) for i in range(ends)])  13.6 us
  transfers between devices with their start and end apart: 18, of which 11 were waited for; matrix products, arithmetic and copies ran while one was open for 0% of the time, Pallas kernels for 0%

commit v1 on v0

v1 whole, which is shorter than its diff:
```python
import numpy as np
import jax
import jax.numpy as jnp
from jax import lax
from jax.experimental import pallas as pl
from jax.experimental.pallas import tpu as pltpu
from jax.sharding import PartitionSpec as P

LEVELS = 3
relax_step = 0.5

PLANES = 5
LANES = 128
RING = PLANES * LANES
EDGE = 32
PAD = 64
ROWHALO = 16
BLOCK = 32


def shifted(shard, axis, by):
    devices = lax.axis_size(axis)
    pairs = [(i, i + by) for i in range(devices) if 0 <= i + by < devices]
    return lax.ppermute(shard, axis, pairs)


def ring_matrices(columns):
    wide = columns + 2 * LANES
    into = np.zeros((wide, RING), np.float32)
    back = np.zeros((RING, columns), np.float32)

    def place(ring):
        return (ring % PLANES) * LANES + ring // PLANES

    for column in range(columns):
        into[column, place(column)] = relax_step
        back[place(column), column] = 1.0
    for quarter in range(LANES // EDGE):
        for i in range(EDGE):
            into[columns + quarter * EDGE + i, place(RING - EDGE + i)] = relax_step
            into[columns + LANES + quarter * EDGE + i, place(columns + i)] = relax_step
    return jnp.asarray(into, jnp.bfloat16), jnp.asarray(back, jnp.bfloat16)


def ring_shift(planes, by):
    out = []
    for k in range(PLANES):
        turns, plane = divmod(k + by, PLANES)
        value = planes[plane]
        if turns:
            value = pltpu.roll(value, (-turns) % LANES, 1)
        out.append(value)
    return out


def add_all(a, b):
    return [x + y for x, y in zip(a, b)]


def smooth_across(planes, dilation):
    for _ in range(2):
        planes = add_all(planes, ring_shift(planes, dilation))
        planes = add_all(planes, ring_shift(planes, -dilation))
    return planes


def smooth_block(ref, start, rows, dilation, scale):
    centre, summed = [], []
    for k in range(PLANES):
        x = [ref[k, pl.ds(start + tap * dilation, rows), :] for tap in range(-2, 3)]
        centre.append(x[2])
        summed.append((x[0] + x[4]) + 4.0 * (x[1] + x[3]) + 6.0 * x[2])
    summed = smooth_across(summed, dilation)
    return centre, [s * w for s, w in zip(summed, scale)]


def limit(values, cut):
    return jnp.minimum(jnp.maximum(values, -cut), cut)


def deblend_kernel(
    scal, thr, own, own_h, near, near_h, far, far_h, top, bot, into, back,
    out, ext, g, c1, c2, f, g2, strip, sem,
):
    seg = own.shape[0]
    columns = own.shape[1]
    window = 2 * seg
    tiles = columns // LANES
    quarter = seg // (LANES // EDGE)
    copies = []

    def bring(src, dst):
        copy = pltpu.make_async_copy(src, dst, sem.at[len(copies)])
        copy.start()
        copies.append(copy)

    for j in range(tiles + 2):
        lanes = pl.ds(j * LANES, LANES)
        bring(top.at[:, lanes], ext.at[j, pl.ds(0, ROWHALO), :])
        bring(bot.at[:, lanes], ext.at[j, pl.ds(ROWHALO + 3 * seg, ROWHALO), :])
    for n, (main, halo) in enumerate(((own, own_h), (near, near_h), (far, far_h))):
        base = ROWHALO + n * seg
        for j in range(tiles):
            bring(main.at[:, pl.ds(j * LANES, LANES)], ext.at[j, pl.ds(base, seg), :])
        for side in range(2):
            for q in range(LANES // EDGE):
                bring(
                    halo.at[pl.ds(side * quarter, quarter), :],
                    ext.at[tiles + side, pl.ds(base + q * quarter, quarter), :],
                )

    offset = scal[0]
    live = scal[8]
    total = scal[11]
    lane = lax.broadcasted_iota(jnp.int32, (1, LANES), 1)
    scale = []
    for k in range(PLANES):
        ring = lane * PLANES + k
        right = jnp.where(scal[13] > 0, 1.0, 0.0)
        left = jnp.where(scal[12] > 0, 1.0, 0.0)
        middle = columns + LANES // 2
        valid = jnp.where(ring < columns, 1.0, jnp.where(ring < middle, right, left))
        scale.append(valid * (1.0 / 256.0))

    zeros = jnp.zeros((PLANES, PAD, LANES), jnp.float32)
    g[:, 0:PAD, :] = zeros
    g[:, PAD + window : 2 * PAD + window, :] = zeros
    for ref in (g2, c1, c2):
        ref[:, 0:PAD, :] = zeros
        ref[:, PAD + window : 2 * PAD + window, :] = zeros
    for copy in copies:
        copy.wait()

    span = window + 2 * ROWHALO
    mm = span // 10

    def permute_in(b, carry):
        start = offset + b * mm
        row = start - ROWHALO + lax.broadcasted_iota(jnp.int32, (mm, 1), 0)
        part = lax.shift_right_arithmetic(row, quarter.bit_length() - 1) & (LANES // EDGE - 1)
        mine = (lane // EDGE) == part
        pieces = [ext[j, pl.ds(start, mm), :] for j in range(tiles)]
        for side in range(2):
            pieces.append(jnp.where(mine, ext[tiles + side, pl.ds(start, mm), :], 0.0))
        lhs = jnp.concatenate([p.astype(jnp.bfloat16) for p in pieces], axis=1)
        result = jnp.dot(lhs, into[...], preferred_element_type=jnp.float32)
        at = pl.multiple_of(PAD - ROWHALO + b * mm, 8)
        for k in range(PLANES):
            g[k, pl.ds(at, mm), :] = result[:, k * LANES : (k + 1) * LANES]
        return carry

    lax.fori_loop(0, 10, permute_in, 0)

    def level_pass(source, target, dilation, first, blocks):
        def body(b, carry):
            at = pl.multiple_of(first + b * BLOCK, 8)
            _, summed = smooth_block(source, at, BLOCK, dilation, scale)
            for k in range(PLANES):
                target[k, pl.ds(at, BLOCK), :] = summed[k]
            return carry

        lax.fori_loop(0, blocks, body, 0)

    def last_pass(base_ref, at, rows):
        centre, summed = smooth_block(c2, at, rows, 4, scale)
        result = []
        for k in range(PLANES):
            x0 = base_ref[k, pl.ds(at, rows), :]
            x1 = c1[k, pl.ds(at, rows), :]
            x2 = centre[k]
            clipped = limit(x0 - x1, thr[0]) + limit(x1 - x2, thr[1]) + limit(x2 - summed[k], thr[2])
            result.append((x0, x0 - clipped))
        return result

    level_pass(g, c1, 1, PAD - ROWHALO, (window + 2 * ROWHALO) // BLOCK)
    level_pass(c1, c2, 2, PAD - ROWHALO, (window + 2 * ROWHALO) // BLOCK)

    def row_factor(t):
        count = jnp.zeros(t.shape, jnp.float32)
        for n in range(5):
            begin, length = scal[1 + n], scal[6 + n]
            count = count + jnp.where((t >= begin) & (t < begin + length), 1.0, 0.0)
        own_live = jnp.where(t < live, 1.0, 0.0)
        inside = jnp.where(t < total, relax_step, 0.0)
        return own_live, own_live * (1.0 - inside * count)

    def f_pass(b, carry):
        at = pl.multiple_of(PAD + b * BLOCK, 8)
        t = b * BLOCK + lax.broadcasted_iota(jnp.int32, (BLOCK, LANES), 0)
        own_live, factor = row_factor(t)
        for k, (x0, value) in enumerate(last_pass(g, at, BLOCK)):
            f[k, pl.ds(at, BLOCK), :] = value
            g2[k, pl.ds(at, BLOCK), :] = own_live * x0 + factor * value
        return carry

    lax.fori_loop(0, window // BLOCK, f_pass, 0)

    half = 32
    rows = 2 * half

    def do_strip(begin, length, at_end, is_own):
        p = begin + (length if at_end else 0)
        t = p - half + lax.broadcasted_iota(jnp.int32, (rows, LANES), 0)
        in_live = jnp.where((t >= begin) & (t < begin + length), 1.0, 0.0)
        in_window = jnp.where((t >= begin) & (t < begin + window), 1.0, 0.0)
        for k in range(PLANES):
            strip[0, k, 16 : 16 + rows, :] = g[k, pl.ds(PAD + p - half, rows), :] * in_live
        for j in range(2):
            _, summed = smooth_block(strip.at[j], 16, rows, 2**j, scale)
            for k in range(PLANES):
                strip[j + 1, k, 16 : 16 + rows, :] = summed[k] * in_window
        mid = 16 + half - 16
        _, summed = smooth_block(strip.at[2], mid, 32, 4, scale)
        t = p - 16 + lax.broadcasted_iota(jnp.int32, (32, LANES), 0)
        shot_live = jnp.where((t >= begin) & (t < begin + length), 1.0, 0.0)
        near_edge = jnp.where((t >= p - 14) & (t < p + 14), shot_live, 0.0)
        own_live = jnp.where((t >= 0) & (t < live), near_edge, 0.0)
        inside = jnp.where(t < total, -relax_step, 0.0)
        weight = own_live * (inside + (1.0 if is_own else 0.0))
        in_window = jnp.where((t >= begin) & (t < begin + window), 1.0, 0.0)
        for k in range(PLANES):
            x0 = strip[0, k, mid : mid + 32, :]
            x1 = strip[1, k, mid : mid + 32, :]
            x2 = strip[2, k, mid : mid + 32, :]
            x3 = summed[k] * in_window
            clipped = limit(x0 - x1, thr[0]) + limit(x1 - x2, thr[1]) + limit(x2 - x3, thr[2])
            where = pl.ds(PAD + p - 16, 32)
            g2[k, where, :] = g2[k, where, :] + weight * (x0 - clipped - f[k, where, :])

    f[:, 0:PAD, :] = zeros
    f[:, PAD + window : 2 * PAD + window, :] = zeros
    strip[:, :, 0:16, :] = jnp.zeros((3, PLANES, 16, LANES), jnp.float32)
    strip[:, :, 16 + rows : 32 + rows, :] = jnp.zeros((3, PLANES, 16, LANES), jnp.float32)
    for n in range(5):
        for at_end in (False, True):
            if n == 0 and not at_end:
                continue
            begin, length = scal[1 + n], scal[6 + n]
            p = begin + (length if at_end else 0)
            low, high = (p - 14, p) if at_end else (p, p + 14)

            @pl.when((length > 0) & (high > 0) & (low < live))
            def _():
                do_strip(begin, length, at_end, n == 2)

    for ref in (c1, c2):
        ref[:, PAD - ROWHALO : PAD, :] = jnp.zeros((PLANES, ROWHALO, LANES), jnp.float32)
        ref[:, PAD + window : PAD + window + ROWHALO, :] = jnp.zeros((PLANES, ROWHALO, LANES), jnp.float32)
    level_pass(g2, c1, 1, PAD, window // BLOCK)
    level_pass(c1, c2, 2, PAD, window // BLOCK)

    def e_pass(b, carry):
        at = pl.multiple_of(PAD + b * BLOCK, 8)
        t = b * BLOCK + lax.broadcasted_iota(jnp.int32, (BLOCK, LANES), 0)
        own_live = jnp.where(t < live, 1.0, 0.0)
        for k, (_, value) in enumerate(last_pass(g2, at, BLOCK)):
            f[k, pl.ds(at, BLOCK), :] = own_live * value
        return carry

    lax.fori_loop(0, window // BLOCK, e_pass, 0)

    mo = 256

    def permute_out(b, carry):
        at = pl.multiple_of(PAD + b * mo, 8)
        high, low = [], []
        for k in range(PLANES):
            x = f[k, pl.ds(at, mo), :]
            h = x.astype(jnp.bfloat16)
            high.append(h)
            low.append((x - h.astype(jnp.float32)).astype(jnp.bfloat16))
        matrix = back[...]
        result = jnp.dot(jnp.concatenate(high, axis=1), matrix, preferred_element_type=jnp.float32)
        result = result + jnp.dot(jnp.concatenate(low, axis=1), matrix, preferred_element_type=jnp.float32)
        out[0, pl.ds(pl.multiple_of(b * mo, 8), mo), :] = result
        return carry

    lax.fori_loop(0, window // mo, permute_out, 0)


def on_device(record, offsets, lengths, thresholds):
    seg, columns = record.shape
    window = 2 * seg
    shots = lax.axis_size("shot")
    rcvs = lax.axis_size("rcv")
    me = lax.axis_index("shot")
    rcv = lax.axis_index("rcv")
    odd = me % 2 == 1
    main = record.astype(jnp.float32)

    quarters = LANES // EDGE

    def pack(edge):
        return edge.reshape(quarters, seg // quarters, EDGE).transpose(1, 0, 2).reshape(seg // quarters, LANES)

    from_left = shifted(pack(main[:, columns - EDGE :]), "rcv", 1)
    from_right = shifted(pack(main[:, :EDGE]), "rcv", -1)
    halo = jnp.concatenate([from_left, from_right], axis=0)

    quarter = seg // quarters
    wide_first = jnp.concatenate([main[:ROWHALO], from_left[:ROWHALO], from_right[:ROWHALO]], axis=1)
    wide_last = jnp.concatenate(
        [main[-ROWHALO:], from_left[quarter - ROWHALO :], from_right[quarter - ROWHALO :]], axis=1
    )
    top = shifted(wide_last, "shot", 1)
    bot = shifted(wide_first, "shot", -3)

    far = shifted(main, "shot", -2)
    far_h = shifted(halo, "shot", -2)
    swap = [(i, i ^ 1) for i in range(shots) if i ^ 1 < shots]
    near = lax.ppermute(jnp.where(odd, main, far), "shot", swap)
    near_h = lax.ppermute(jnp.where(odd, halo, far_h), "shot", swap)

    mine = jnp.stack([offsets[0], lengths[0]])
    pairs = [shifted(mine, "shot", -by) if by else mine for by in range(-2, 3)]
    begins = [by * seg + pair[0] - offsets[0] for by, pair in zip(range(-2, 3), pairs)]
    total = shots * seg - me * seg - offsets[0]
    scal = jnp.stack(
        [offsets[0]] + begins + [pair[1] for pair in pairs]
        + [total, (rcv > 0).astype(jnp.int32), (rcv < rcvs - 1).astype(jnp.int32)]
    )
    into, back = ring_matrices(columns)
    deep = window + 2 * PAD
    work = pltpu.VMEM((PLANES, deep, LANES), jnp.float32)
    smem = pl.BlockSpec(memory_space=pltpu.SMEM)
    anywhere = pl.BlockSpec(memory_space=pl.ANY)
    vmem = pl.BlockSpec(memory_space=pltpu.VMEM)
    return pl.pallas_call(
        deblend_kernel,
        out_shape=jax.ShapeDtypeStruct((1, window, columns), jnp.float32),
        in_specs=[smem, smem] + [anywhere] * 8 + [vmem, vmem],
        out_specs=vmem,
        scratch_shapes=[
            pltpu.VMEM((columns // LANES + 2, 3 * seg + 2 * ROWHALO, LANES), jnp.float32),
            work, work, work, work, work,
            pltpu.VMEM((3, PLANES, 96, LANES), jnp.float32),
            pltpu.SemaphoreType.DMA((64,)),
        ],
        compiler_params=pltpu.CompilerParams(vmem_limit_bytes=60 * 1024 * 1024),
    )(scal, thresholds, main, halo, near, near_h, far, far_h, top, bot, into, back)


def solution(mesh):
    return jax.shard_map(
        on_device,
        mesh=mesh,
        in_specs=(P("shot", "rcv"), P("shot"), P("shot"), P()),
        out_specs=P("shot", None, "rcv"),
        check_vma=False,
    )
```

time: 439 us -> 264 us (0.60)
  the two profiles are of different devices: /device:TPU:9 before, /device:TPU:13 now
where the time goes in v1:
time: 264 us; the launch traced here: 262 us
  Pallas kernels  134 us (51%)
  waiting for transfers between devices  78.3 us (30%)
  starting transfers between devices  35.3 us (13%)
  local copies, waits for them, and re-layouts  6.93 us (3%)
  between operations  4.14 us (2%)
  other arithmetic  3.35 us (1%)
    pallas_call x1, Pallas kernels, on_device(): pl.pallas_call(deblend_kernel, out_shape=jax.ShapeDtypeStruct((1, window,...  134 us
    ppermute x10, waiting for transfers between devices, shifted(): return lax.ppermute(shard, axis, pairs)  78.3 us
    ppermute x10, starting transfers between devices, shifted(): return lax.ppermute(shard, axis, pairs)  31.2 us
  transfers between devices with their start and end apart: 12, of which 4 were waited for; matrix products, arithmetic and copies ran while one was open for 2% of the time, Pallas kernels for 0%

profile of v1, /device:TPU:13, one launch (start us, length us, event | category | flops | bytes accessed | tf_op | source)
XLA Modules:
  0.0 261.8 jit_solution(10921957702173094185)
XLA Ops:
  0.0 1.6 convert_element_type.2.own
  1.6 2.1 collective-permute-start.6
  5.0 45.1 %collective-permute-done.6.far = f32[1024,512]{1,0:T(8,128)} collective-permute-done((f32[1024,512]{1,0:T(8,128)S(1)}, f32[1024,512]{1,0:T(8,128)}, u32[]{:S(2)}, u32[]{:S(2)}) %collective-permute-start.6) | collective-permute-done | bytes 2097184 | tf_op jit(solution)/shard_map/ppermute | solution.py:24
  50.1 1.6 broadcast_select_fusion
  51.8 1.8 collective-permute-start.7
  53.6 0.1 pad_add_fusion
  53.7 2.2 collective-permute-start.3
  55.9 1.9 collective-permute-start.2
  57.8 4.3 %collective-permute-start.1 = (s32[2]{0:T(128)S(1)}, s32[2]{0:T(128)S(1)}, u32[]{:S(2)}, u32[]{:S(2)}) collective-permute-start(s32[2]{0:T(128)S(1)} %pad_add_fusion), channel_id=1, source_target_pairs={{0,4},{4,8},{8,12},{12,16},{16,20},{20,24},{24,28},{1,5},{5,9},{9,... | collective-permute-start | bytes 32 | tf_op jit(solution)/shard_map/ppermute | solution.py:24
  62.1 3.0 %collective-permute-start = (s32[2]{0:T(128)S(1)}, s32[2]{0:T(128)S(1)}, u32[]{:S(2)}, u32[]{:S(2)}) collective-permute-start(s32[2]{0:T(128)S(1)} %pad_add_fusion), channel_id=1, source_target_pairs={{0,8},{4,12},{8,16},{12,20},{16,24},{20,28},{1,9},{5,13},{9,17},{1... | collective-permute-start | bytes 32 | tf_op jit(solution)/shard_map/ppermute | solution.py:24
  65.1 0.1 fusion.1
  65.3 0.2 copy.11
  65.5 0.1 copy.12
  65.6 0.2 copy.9
  65.7 0.1 copy.10
  65.9 6.0 %collective-permute-start.4 = (f32[256,128]{1,0:T(8,128)S(1)}, f32[256,128]{1,0:T(8,128)S(1)}, u32[]{:S(2)}, u32[]{:S(2)}) collective-permute-start(f32[256,128]{1,0:T(8,128)S(1)} %copy.10), channel_id=1, source_target_pairs={{0,1},{1,2},{2,3},{4,5},{5,6},{6,7},{8,9},{9,10},{10,11},{12,13},{... | collective-permute-start | bytes 393224 | tf_op jit(solution)/shard_map/ppermute | solution.py:24
  71.8 0.6 fusion.4
  72.4 24.9 %collective-permute-done.2 = s32[2]{0:T(128)S(1)} collective-permute-done((s32[2]{0:T(128)S(1)}, s32[2]{0:T(128)S(1)}, u32[]{:S(2)}, u32[]{:S(2)}) %collective-permute-start.2) | collective-permute-done | bytes 40 | tf_op jit(solution)/shard_map/ppermute | solution.py:24
  97.3 4.4 %collective-permute-start.5 = (f32[256,128]{1,0:T(8,128)S(1)}, f32[256,128]{1,0:T(8,128)S(1)}, u32[]{:S(2)}, u32[]{:S(2)}) collective-permute-start(f32[256,128]{1,0:T(8,128)S(1)} %copy.12), channel_id=1, source_target_pairs={{1,0},{2,1},{3,2},{5,4},{6,5},{7,6},{9,8},{10,9},{11,10},{13,12},{... | collective-permute-start | bytes 393224 | tf_op jit(solution)/shard_map/ppermute | solution.py:24
  101.7 0.7 fusion.5
  102.3 0.6 fusion.6
  102.9 2.5 collective-permute-done.5
  105.4 2.1 collective-permute-start.8
  107.5 5.9 %collective-permute-done.8.far_h = f32[512,128]{1,0:T(8,128)S(1)} collective-permute-done((f32[512,128]{1,0:T(8,128)S(1)}, f32[512,128]{1,0:T(8,128)S(1)}, u32[]{:S(2)}, u32[]{:S(2)}) %collective-permute-start.8) | collective-permute-done | bytes 262176 | tf_op jit(solution)/shard_map/ppermute | solution.py:24
  113.4 2.3 collective-permute-start.9
  115.7 2.9 %collective-permute-start.10 = (f32[16,768]{1,0:T(8,128)S(1)}, f32[16,768]{1,0:T(8,128)S(1)}, u32[]{:S(2)}, u32[]{:S(2)}) collective-permute-start(f32[16,768]{1,0:T(8,128)S(1)} %pad_maximum_fusion), channel_id=1, source_target_pairs={{0,4},{4,8},{8,12},{12,16},{16,20},{20,24},{24,28},{1,5},{5,9},{9,... | collective-permute-start | bytes 147464 | tf_op jit(solution)/shard_map/ppermute | solution.py:24
  118.7 2.4 collective-permute-start.11
  121.0 0.6 fusion.7
  124.2 3.1 %stack.44.scal = s32[14]{0:T(128)} concatenate(s32[1]{0:T(128)} %copy.14, s32[1]{0:T(128)} %bitcast.2, s32[1]{0:T(128)} %bitcast.4, s32[1]{0:T(128)} %constant.36.clone.1, s32[1]{0:T(128)} %bitcast.6, s32[1]{0:T(128)} %bitcast.8, s32[1]{0:T(128)} %get-tuple-element.19, s32[1]{0:T(128)} %get-tuple-element.17, s32[1]{0:T(128)S(6)} %copy.15, s32[1]{0:T(128)} %get-tuple-element.15, ...), dimensions={0} | concatenate | bytes 112 | tf_op jit(solution)/shard_map/stack | solution.py:318
  127.4 0.5 copy-done.5
  128.0 0.1 copy-done.4
  128.1 133.8 %shard_map.64 = f32[1,2048,512]{2,1,0:T(8,128)} custom-call(s32[14]{0:T(128)} %stack.44.scal, f32[3]{0:T(128)} %thr.1, f32[1024,512]{1,0:T(8,128)} %copy-done.1, f32[512,128]{1,0:T(8,128)} %copy-done.2, f32[1024,512]{1,0:T(8,128)} %collective-permute-done.7.near, f32[512,128]{1,0:T(8,128)} %copy-done.4, f32[1024,512]{1,0:T(8,128)} %collective-permute-done.6.far, ...), custom_call_target="tpu_custom_call" | custom-call | tf_op jit(solution)/shard_map/pallas_call | solution.py:328
  (28 shorter events, 0.1 us)
Async XLA Ops:
  0.0 50.1 %copy-start = (bf16[1024,512]{1,0:T(8,128)(2,1)S(1)}, bf16[1024,512]{1,0:T(8,128)(2,1)}, u32[]{:S(2)}) copy-start(bf16[1024,512]{1,0:T(8,128)(2,1)} %param.6) | copy-start | bytes 3145732
  1.6 50.2 %copy-start.1 = (f32[1024,512]{1,0:T(8,128)}, f32[1024,512]{1,0:T(8,128)S(1)}, u32[]{:S(2)}) copy-start(f32[1024,512]{1,0:T(8,128)S(1)} %convert_element_type.2.own) | copy-start | bytes 6291460
  1.6 48.5 %collective-permute-start.6 = (f32[1024,512]{1,0:T(8,128)S(1)}, f32[1024,512]{1,0:T(8,128)}, u32[]{:S(2)}, u32[]{:S(2)}) collective-permute-start(f32[1024,512]{1,0:T(8,128)S(1)} %convert_element_type.2.own), channel_id=1, source_target_pairs={{8,0},{12,4},{16,8},{20,12},{24,16},{28,20},{9,1},{13,5},{17,9},{2... | collective-permute-start | bytes 6291464 | tf_op jit(solution)/shard_map/ppermute | solution.py:24
  51.8 75.6 %collective-permute-start.7 = (f32[1024,512]{1,0:T(8,128)}, f32[1024,512]{1,0:T(8,128)}, u32[]{:S(2)}, u32[]{:S(2)}) collective-permute-start(f32[1024,512]{1,0:T(8,128)} %broadcast_select_fusion), channel_id=1, source_target_pairs={{0,4},{4,0},{8,12},{12,8},{16,20},{20,16},{24,28},{28,24},{1,5},{5... | collective-permute-start | bytes 6291464 | tf_op jit(solution)/shard_map/ppermute | solution.py:311
  53.7 12.2 %collective-permute-start.3 = (s32[2]{0:T(128)S(1)}, s32[2]{0:T(128)S(1)}, u32[]{:S(2)}, u32[]{:S(2)}) collective-permute-start(s32[2]{0:T(128)S(1)} %pad_add_fusion), channel_id=1, source_target_pairs={{8,0},{12,4},{16,8},{20,12},{24,16},{28,20},{9,1},{13,5},{17,9},{2... | collective-permute-start | bytes 32 | tf_op jit(solution)/shard_map/ppermute | solution.py:24
  55.9 41.4 %collective-permute-start.2 = (s32[2]{0:T(128)S(1)}, s32[2]{0:T(128)S(1)}, u32[]{:S(2)}, u32[]{:S(2)}) collective-permute-start(s32[2]{0:T(128)S(1)} %pad_add_fusion), channel_id=1, source_target_pairs={{4,0},{8,4},{12,8},{16,12},{20,16},{24,20},{28,24},{5,1},{9,5},{13... | collective-permute-start | bytes 32 | tf_op jit(solution)/shard_map/ppermute | solution.py:24
  57.8 44.5 %collective-permute-start.1 = (s32[2]{0:T(128)S(1)}, s32[2]{0:T(128)S(1)}, u32[]{:S(2)}, u32[]{:S(2)}) collective-permute-start(s32[2]{0:T(128)S(1)} %pad_add_fusion), channel_id=1, source_target_pairs={{0,4},{4,8},{8,12},{12,16},{16,20},{20,24},{24,28},{1,5},{5,9},{9,... | collective-permute-start | bytes 32 | tf_op jit(solution)/shard_map/ppermute | solution.py:24
  62.1 59.0 %collective-permute-start = (s32[2]{0:T(128)S(1)}, s32[2]{0:T(128)S(1)}, u32[]{:S(2)}, u32[]{:S(2)}) collective-permute-start(s32[2]{0:T(128)S(1)} %pad_add_fusion), channel_id=1, source_target_pairs={{0,8},{4,12},{8,16},{12,20},{16,24},{20,28},{1,9},{5,13},{9,17},{1... | collective-permute-start | bytes 32 | tf_op jit(solution)/shard_map/ppermute | solution.py:24
  65.9 37.0 %collective-permute-start.4 = (f32[256,128]{1,0:T(8,128)S(1)}, f32[256,128]{1,0:T(8,128)S(1)}, u32[]{:S(2)}, u32[]{:S(2)}) collective-permute-start(f32[256,128]{1,0:T(8,128)S(1)} %copy.10), channel_id=1, source_target_pairs={{0,1},{1,2},{2,3},{4,5},{5,6},{6,7},{8,9},{9,10},{10,11},{12,13},{... | collective-permute-start | bytes 393224 | tf_op jit(solution)/shard_map/ppermute | solution.py:24
  97.3 8.1 %collective-permute-start.5 = (f32[256,128]{1,0:T(8,128)S(1)}, f32[256,128]{1,0:T(8,128)S(1)}, u32[]{:S(2)}, u32[]{:S(2)}) collective-permute-start(f32[256,128]{1,0:T(8,128)S(1)} %copy.12), channel_id=1, source_target_pairs={{1,0},{2,1},{3,2},{5,4},{6,5},{7,6},{9,8},{10,9},{11,10},{13,12},{... | collective-permute-start | bytes 393224 | tf_op jit(solution)/shard_map/ppermute | solution.py:24
  105.4 22.0 %copy-start.2 = (f32[512,128]{1,0:T(8,128)}, f32[512,128]{1,0:T(8,128)S(1)}, u32[]{:S(2)}) copy-start(f32[512,128]{1,0:T(8,128)S(1)} %constant_dynamic-update-slice_fusion.own_h) | copy-start | bytes 786436
  105.4 8.0 %collective-permute-start.8 = (f32[512,128]{1,0:T(8,128)S(1)}, f32[512,128]{1,0:T(8,128)S(1)}, u32[]{:S(2)}, u32[]{:S(2)}) collective-permute-start(f32[512,128]{1,0:T(8,128)S(1)} %constant_dynamic-update-slice_fusion.own_h), channel_id=1, source_target_pairs={{8,0},{12,4},{16,8},{20,12},{24,16},{28,20},{9,1},{13,5},{17,9},{2... | collective-permute-start | bytes 786440 | tf_op jit(solution)/shard_map/ppermute | solution.py:24
  113.4 14.0 %copy-start.3 = (f32[512,128]{1,0:T(8,128)}, f32[512,128]{1,0:T(8,128)S(1)}, u32[]{:S(2)}) copy-start(f32[512,128]{1,0:T(8,128)S(1)} %collective-permute-done.8.far_h) | copy-start | bytes 786436
  113.4 13.9 %collective-permute-start.9 = (f32[512,128]{1,0:T(8,128)S(1)}, f32[512,128]{1,0:T(8,128)S(1)}, u32[]{:S(2)}, u32[]{:S(2)}) collective-permute-start(f32[512,128]{1,0:T(8,128)S(1)} %broadcast_select_fusion.1), channel_id=1, source_target_pairs={{0,4},{4,0},{8,12},{12,8},{16,20},{20,16},{24,28},{28,24},{1,5},{5... | collective-permute-start | bytes 786440 | tf_op jit(solution)/shard_map/ppermute | solution.py:312
  115.7 11.6 %collective-permute-start.10 = (f32[16,768]{1,0:T(8,128)S(1)}, f32[16,768]{1,0:T(8,128)S(1)}, u32[]{:S(2)}, u32[]{:S(2)}) collective-permute-start(f32[16,768]{1,0:T(8,128)S(1)} %pad_maximum_fusion), channel_id=1, source_target_pairs={{0,4},{4,8},{8,12},{12,16},{16,20},{20,24},{24,28},{1,5},{5,9},{9,... | collective-permute-start | bytes 147464 | tf_op jit(solution)/shard_map/ppermute | solution.py:24
  118.7 8.7 %collective-permute-start.11 = (f32[16,768]{1,0:T(8,128)S(1)}, f32[16,768]{1,0:T(8,128)S(1)}, u32[]{:S(2)}, u32[]{:S(2)}) collective-permute-start(f32[16,768]{1,0:T(8,128)S(1)} %pad_maximum_fusion.1), channel_id=1, source_target_pairs={{12,0},{16,4},{20,8},{24,12},{28,16},{13,1},{17,5},{21,9},{25,13},... | collective-permute-start | bytes 147464 | tf_op jit(solution)/shard_map/ppermute | solution.py:24
  127.3 0.6 copy-start.5
  127.3 0.6 copy-start.6
  127.3 0.7 copy-start.4

commit v2 on v0

v2 whole, which is shorter than its diff:
```python
import functools

import numpy as np
import jax
import jax.numpy as jnp
from jax import lax
from jax.experimental import pallas as pl
from jax.experimental.pallas import tpu as pltpu
from jax.sharding import PartitionSpec as P

LEVELS = 3
relax_step = 0.5

PLANES = 5
LANES = 128
RING = PLANES * LANES
EDGE = 32
QUARTERS = LANES // EDGE
HEAD = 128
PAD = 64
ROWHALO = 16
BLOCK = 64
STRIP = 64


def shifted(shard, axis, by):
    devices = lax.axis_size(axis)
    pairs = [(i, i + by) for i in range(devices) if 0 <= i + by < devices]
    return lax.ppermute(shard, axis, pairs)


def ring_matrices(columns):
    wide = columns + 2 * LANES
    into = np.zeros((wide, RING), np.float32)
    back = np.zeros((RING, columns), np.float32)

    def place(ring):
        return (ring % PLANES) * LANES + ring // PLANES

    for column in range(columns):
        into[column, place(column)] = relax_step
        back[place(column), column] = 1.0
    for quarter in range(LANES // EDGE):
        for i in range(EDGE):
            into[columns + quarter * EDGE + i, place(RING - EDGE + i)] = relax_step
            into[columns + LANES + quarter * EDGE + i, place(columns + i)] = relax_step
    return jnp.asarray(into, jnp.bfloat16), jnp.asarray(back, jnp.bfloat16)


def smooth_across(planes, dilation):
    rolled = {}

    def at(position):
        turns, plane = divmod(position, PLANES)
        if turns == 0:
            return planes[plane]
        if (turns, plane) not in rolled:
            rolled[turns, plane] = pltpu.roll(planes[plane], (-turns) % LANES, 1)
        return rolled[turns, plane]

    return [
        (at(k - 2 * dilation) + at(k + 2 * dilation))
        + 4.0 * (at(k - dilation) + at(k + dilation))
        + 6.0 * planes[k]
        for k in range(PLANES)
    ]


def limit(values, cut):
    return jnp.minimum(jnp.maximum(values, -cut), cut)


def blocks_of(first, count, body):
    def step(b, carry):
        at = pl.multiple_of(first + b * (2 * BLOCK), 8)
        body(at, BLOCK)
        body(pl.multiple_of(at + BLOCK, 8), BLOCK)
        return carry

    lax.fori_loop(0, count // 2, step, 0)

    @pl.when(count % 2 == 1)
    def _():
        body(pl.multiple_of(first + (count - 1) * BLOCK, 8), BLOCK)


def smooth_block(ref, start, rows, dilation, scale):
    centre, summed = [], []
    for k in range(PLANES):
        x = [ref[k, pl.ds(start + tap * dilation, rows), :] for tap in range(-2, 3)]
        centre.append(x[2])
        summed.append((x[0] + x[4]) + 4.0 * (x[1] + x[3]) + 6.0 * x[2])
    summed = smooth_across(summed, dilation)
    return centre, [s * w for s, w in zip(summed, scale)]


def deblend_kernel(geometry, pieces, span, aliased, params, thr, into, back, *refs):
    seg, columns, arrays = geometry
    refs = refs[:arrays] + refs[arrays + aliased :]
    sources = refs[:arrays]
    out, g, c1, c2, f, g2, strip, staged, sem = refs[arrays:]
    window = 2 * seg
    quarter_rows = seg // QUARTERS

    shots = lax.axis_size("shot")
    me = lax.axis_index("shot")
    rcv = lax.axis_index("rcv")
    offset = params[2, 0]
    live = params[2, 1]
    total = (shots - me) * seg - offset

    def shot(by):
        return by * seg + params[by + 2, 0] - offset, params[by + 2, 1]

    low, count = span(offset)
    low = pl.multiple_of(low, 8)
    high = low + count * BLOCK

    lane = lax.broadcasted_iota(jnp.int32, (1, LANES), 1)
    has_right = jnp.where(rcv < lax.axis_size("rcv") - 1, 1.0, 0.0)
    has_left = jnp.where(rcv > 0, 1.0, 0.0)
    scale = []
    for k in range(PLANES):
        ring = lane * PLANES + k
        side = jnp.where(ring < columns + LANES // 2, has_right, has_left)
        scale.append(jnp.where(ring < columns, 1.0, side) * (1.0 / 256.0))

    def permute_in(main, halo, first, rows, quarter, row):
        lhs = [sources[main][pl.ds(first, rows), 0:columns].astype(jnp.bfloat16)]
        mine = (lane // EDGE) == quarter
        for side in range(2):
            if halo is None:
                part = sources[main][0:rows, columns + side * LANES : columns + (side + 1) * LANES]
            else:
                inner, part = row % quarter_rows, []
                while inner < row % quarter_rows + rows:
                    at = (2 * side + inner // HEAD) * LANES
                    end = min(inner // HEAD * HEAD + HEAD, row % quarter_rows + rows)
                    part.append(sources[halo][inner % HEAD : inner % HEAD + end - inner, at : at + LANES])
                    inner = end
                part = jnp.concatenate(part, axis=0)
            lhs.append(jnp.where(mine, part, 0.0).astype(jnp.bfloat16))
        result = jnp.dot(jnp.concatenate(lhs, axis=1), into[...], preferred_element_type=jnp.float32)
        for k in range(PLANES):
            g[k, PAD + row : PAD + row + rows, :] = result[:, k * LANES : (k + 1) * LANES]

    for parity, *piece in pieces:
        rows, row = piece[3], piece[5]
        wanted = (count > 0) & (row < offset + high + 40) & (row + rows > offset + low - 40)
        if parity is not None:
            wanted = wanted & (lax.rem(me, 2) == parity)

        @pl.when(wanted)
        def _():
            permute_in(*piece)

    def level_pass(source, shift, target, dilation, first, count):
        def body(at, rows):
            _, summed = smooth_block(source, at + shift, rows, dilation, scale)
            for k in range(PLANES):
                target[k, pl.ds(at, rows), :] = summed[k]

        blocks_of(first, count, body)

    def last_pass(base_ref, shift, at, rows):
        centre, summed = smooth_block(c2, at, rows, 4, scale)
        for k in range(PLANES):
            x0 = base_ref[k, pl.ds(at + shift, rows), :]
            x1 = c1[k, pl.ds(at, rows), :]
            x2 = centre[k]
            clipped = limit(x0 - x1, thr[0]) + limit(x1 - x2, thr[1]) + limit(x2 - summed[k], thr[2])
            yield k, x0, x0 - clipped

    def f_pass(at, rows):
        t = at - PAD + lax.broadcasted_iota(jnp.int32, (rows, LANES), 0)
        count = jnp.zeros(t.shape, jnp.float32)
        for by in range(-2, 3):
            begin, length = shot(by)
            count = count + jnp.where((t >= begin) & (t < begin + length), 1.0, 0.0)
        own_live = jnp.where((t >= 0) & (t < live), 1.0, 0.0)
        inside = jnp.where(t < total, relax_step, 0.0)
        factor = own_live * (1.0 - inside * count)
        for k, x0, value in last_pass(g, offset, at, rows):
            f[k, pl.ds(at, rows), :] = value
            g2[k, pl.ds(at, rows), :] = own_live * x0 + factor * value

    half = STRIP // 2

    def do_strip(by, at_end):
        begin, length = shot(by)
        p = begin + jnp.where(at_end, length, 0)
        t = p - half + lax.broadcasted_iota(jnp.int32, (STRIP, LANES), 0)
        in_live = jnp.where((t >= begin) & (t < begin + length), 1.0, 0.0)
        in_window = jnp.where((t >= begin) & (t < begin + window), 1.0, 0.0)
        for k in range(PLANES):
            strip[0, k, 16 : 16 + STRIP, :] = g[k, pl.ds(PAD + offset + p - half, STRIP), :] * in_live
        for j in range(2):
            _, summed = smooth_block(strip.at[j], 16, STRIP, 2**j, scale)
            for k in range(PLANES):
                strip[j + 1, k, 16 : 16 + STRIP, :] = summed[k] * in_window
        mid = half
        _, summed = smooth_block(strip.at[2], mid, 32, 4, scale)
        t = p - 16 + lax.broadcasted_iota(jnp.int32, (32, LANES), 0)
        in_window = jnp.where((t >= begin) & (t < begin + window), 1.0, 0.0)
        near_edge = (t >= begin) & (t < begin + length) & (t >= p - 14) & (t < p + 14)
        own_live = (t >= 0) & (t < live)
        inside = jnp.where(t < total, -relax_step, 0.0)
        weight = jnp.where(near_edge & own_live, inside + jnp.where(by == 0, 1.0, 0.0), 0.0)
        for k in range(PLANES):
            x0 = strip[0, k, mid : mid + 32, :]
            x1 = strip[1, k, mid : mid + 32, :]
            x2 = strip[2, k, mid : mid + 32, :]
            x3 = summed[k] * in_window
            clipped = limit(x0 - x1, thr[0]) + limit(x1 - x2, thr[1]) + limit(x2 - x3, thr[2])
            where = pl.ds(PAD + p - 16, 32)
            g2[k, where, :] = g2[k, where, :] + weight * (x0 - clipped - f[k, where, :])

    def e_pass(at, rows):
        t = at - PAD + lax.broadcasted_iota(jnp.int32, (rows, LANES), 0)
        own_live = jnp.where(t < live, 1.0, 0.0)
        for k, _, value in last_pass(g2, 0, at, rows):
            f[k, pl.ds(at, rows), :] = own_live * value

    def permute_out(at, rows):
        high, low = [], []
        for k in range(PLANES):
            x = f[k, pl.ds(at, rows), :]
            h = x.astype(jnp.bfloat16)
            high.append(h)
            low.append((x - h.astype(jnp.float32)).astype(jnp.bfloat16))
        both = jnp.concatenate([jnp.concatenate(high, axis=1), jnp.concatenate(low, axis=1)], axis=0)
        result = jnp.dot(both, back[...], preferred_element_type=jnp.float32)
        staged[pl.ds(pl.multiple_of(at - PAD, 8), rows), :] = result[:rows] + result[rows:]

    def clear_edges(ref):
        ref[:, PAD - 16 : PAD, :] = jnp.zeros((PLANES, 16, LANES), jnp.float32)
        ref[:, PAD + window : PAD + window + 16, :] = jnp.zeros((PLANES, 16, LANES), jnp.float32)

    strip[:, :, 0:16, :] = jnp.zeros((3, PLANES, 16, LANES), jnp.float32)
    strip[:, :, 16 + STRIP : 32 + STRIP, :] = jnp.zeros((3, PLANES, 16, LANES), jnp.float32)

    def process():
        first = PAD + low
        outer, many = first - BLOCK // 2, count + 1
        level_pass(g, offset, c1, 1, outer, many)
        level_pass(c1, 0, c2, 2, outer, many)
        blocks_of(outer, many, f_pass)

        def strip_step(i, carry):
            by, at_end = i // 2 - 2, i % 2 == 1
            begin, length = shot(by)
            p = begin + jnp.where(at_end, length, 0)
            begins_at = jnp.where(at_end, p - 14, p)
            bottom = jnp.maximum(low - 14, 0)
            top = jnp.minimum(high + 14, live)

            @pl.when((length > 0) & (begins_at + 14 > bottom) & (begins_at < top))
            def _():
                do_strip(by, at_end)

            return carry

        lax.fori_loop(1, 10, strip_step, 0)
        clear_edges(g2)
        level_pass(g2, 0, c1, 1, outer, many)
        clear_edges(c1)
        level_pass(c1, 0, c2, 2, outer, many)
        clear_edges(c2)
        blocks_of(first, count, e_pass)
        blocks_of(first, count, permute_out)

        def copy(i):
            rows = pl.ds(pl.multiple_of(low + i * BLOCK, 8), BLOCK)
            return pltpu.make_async_copy(staged.at[rows, :], out.at[0, rows, :], sem.at[i])

        def start(i, carry):
            copy(i).start()
            return carry

        def wait(i, carry):
            copy(i).wait()
            return carry

        lax.fori_loop(0, count, start, 0)
        lax.fori_loop(0, count, wait, 0)

    @pl.when(count > 0)
    def _():
        process()


def prepare_kernel(record, first_edge, last_edge):
    seg, columns = record.shape
    quarter = seg // QUARTERS
    lane = lax.broadcasted_iota(jnp.int32, (1, LANES), 1)
    for out, start, inner in ((first_edge, 0, 0), (last_edge, columns - LANES, LANES - EDGE)):
        packed = jnp.zeros((quarter, LANES), jnp.float32)
        for q in range(QUARTERS):
            rows = record[q * quarter : (q + 1) * quarter, start : start + LANES].astype(jnp.float32)
            turn = (q * EDGE - inner) % LANES
            packed = jnp.where(lane // EDGE == q, pltpu.roll(rows, turn, 1) if turn else rows, packed)
        out[...] = packed


def header_kernel(parts, offsets, lengths, record, left, right, wide_first, wide_last, *own):
    seg, columns = record.shape
    quarter = seg // QUARTERS
    lane = lax.broadcasted_iota(jnp.int32, (8, LANES), 1)
    about = jnp.where(lane == 0, offsets[0], jnp.where(lane == 1, lengths[0], 0)).astype(jnp.float32)
    first = own[0]
    for side, halo in enumerate((left, right)):
        for part in range(quarter // HEAD):
            at = (2 * side + part) * LANES
            first[0:HEAD, at : at + LANES] = halo[part * HEAD : (part + 1) * HEAD, :]
    first[HEAD : HEAD + 8, :] = jnp.concatenate([about] * (columns // LANES), axis=1)
    first[HEAD + 8 :, :] = record[0 : parts[1], :].astype(jnp.float32)
    for k in range(1, len(own)):
        own[k][...] = record[parts[k] : parts[k + 1], :].astype(jnp.float32)
    wide_first[:, 0:columns] = record[0:ROWHALO, :].astype(jnp.float32)
    wide_last[0:ROWHALO, 0:columns] = record[seg - ROWHALO : seg, :].astype(jnp.float32)
    for side, halo in enumerate((left, right)):
        at = columns + side * LANES
        wide_first[:, at : at + LANES] = halo[0:ROWHALO, :]
        wide_last[0:ROWHALO, at : at + LANES] = halo[quarter - ROWHALO : quarter, :]
    wide_last[ROWHALO:, :] = jnp.concatenate([about] * (columns // LANES + 2), axis=1)


def on_device(record, offsets, lengths, thresholds):
    seg, columns = record.shape
    window = 2 * seg
    shots = lax.axis_size("shot")
    q = seg // QUARTERS
    skip = HEAD + 8
    step = (seg + skip + 4 * 16 - 1) // (4 * 16) * 16
    parts = [0] + [seg - k * step for k in (3, 2, 1, 0)]
    swap = [(i, i ^ 1) for i in range(shots) if i ^ 1 < shots]
    smem = pl.BlockSpec(memory_space=pltpu.SMEM)
    anywhere = pl.BlockSpec(memory_space=pl.ANY)
    vmem = pl.BlockSpec(memory_space=pltpu.VMEM)

    def array(*shape):
        return jax.ShapeDtypeStruct(shape, jnp.float32)

    def part(k):
        return array(parts[k + 1] - parts[k] + (skip if k == 0 else 0), columns)

    first_edge, last_edge = pl.pallas_call(
        prepare_kernel, out_shape=(array(q, LANES), array(q, LANES)), in_specs=[vmem], out_specs=(vmem, vmem)
    )(record)
    from_left = shifted(last_edge, "rcv", 1)
    from_right = shifted(first_edge, "rcv", -1)
    mine = jnp.concatenate([offsets, lengths]).astype(jnp.float32)
    wide = columns + 2 * LANES
    wide_first, wide_last, *own = pl.pallas_call(
        functools.partial(header_kernel, parts),
        out_shape=(array(ROWHALO, wide), array(ROWHALO + 8, wide)) + tuple(part(k) for k in range(4)),
        in_specs=[smem, smem, vmem, vmem, vmem],
        out_specs=(vmem,) * 6,
    )(offsets, lengths, record, from_left, from_right)
    to_odd = [(i, i + 1) for i in range(0, shots - 1, 2)]
    to_even = [(i + 1, i) for i in range(0, shots - 1, 2)]
    far = [shifted(x, "shot", -2) for x in own]
    passed = [lax.ppermute(x, "shot", to_odd) for x in far]
    given = [lax.ppermute(x, "shot", to_even) for x in own]
    second_last = shifted(mine, "shot", 2)
    top = shifted(wide_last, "shot", 1)
    bot = shifted(wide_first, "shot", -3)
    about = [second_last, top[ROWHALO, :2], mine, passed[0][HEAD, :2] + given[0][HEAD, :2], far[0][HEAD, :2]]
    params = jnp.stack(about).astype(jnp.int32)

    into, back = ring_matrices(columns)
    deep = window + 2 * PAD
    work = pltpu.VMEM((PLANES, deep, LANES), jnp.float32)

    def phase(out, arrays, waits, pieces, span):
        held = waits if out is None else [out] + waits
        return pl.pallas_call(
            functools.partial(deblend_kernel, (seg, columns, len(arrays)), pieces, span, len(held)),
            out_shape=array(1, window, columns),
            in_specs=[smem, smem, vmem, vmem] + [vmem] * len(arrays) + [anywhere] * len(held),
            out_specs=anywhere,
            input_output_aliases={} if out is None else {4 + len(arrays): 0},
            scratch_shapes=[
                pltpu.VMEM((PLANES, 3 * seg + 2 * PAD, LANES), jnp.float32),
                work, work, work, work,
                pltpu.VMEM((3, PLANES, STRIP + 32, LANES), jnp.float32),
                pltpu.VMEM((window, columns), jnp.float32),
                pltpu.SemaphoreType.DMA((window // BLOCK,)),
            ],
            compiler_params=pltpu.CompilerParams(vmem_limit_bytes=60 * 1024 * 1024),
        )(params, thresholds, into, back, *arrays, *held)

    def pieces_of(main, halo, segment, begin, end, start=0, parity=None):
        found = []
        while begin < end:
            quarter = begin // q
            until = min(end, (quarter + 1) * q)
            found.append((parity, main, halo, begin - start, until - begin, quarter, segment * seg + begin))
            begin = until
        return found

    def part_pieces(k, main, halo, segment, begin=None, end=None, parity=None):
        start = parts[k] - (skip if k == 0 else 0)
        begin = parts[k] if begin is None else begin
        return pieces_of(main, halo, segment, begin, parts[k + 1] if end is None else end, start, parity)

    blocks = window // BLOCK

    def mark(offset, rows):
        return jnp.clip((seg + rows - 28 - offset) // BLOCK, 0, blocks)

    def far_begin(offset):
        return jnp.minimum((2 * seg + 35 - offset) // 8 * 8 // BLOCK, blocks)

    def far_middle(offset):
        return jnp.clip((2 * seg + parts[2] - 28 - offset) // BLOCK, far_begin(offset), blocks)


    def takes_far(offset):
        return far_middle(offset) - far_begin(offset) >= 4

    def second(offset):
        near_count = mark(offset, 0)
        far_count = far_middle(offset) - far_begin(offset)
        is_far = takes_far(offset)
        return jnp.where(is_far, far_begin(offset), 0) * BLOCK, jnp.where(is_far, far_count, near_count)

    def third(offset):
        begin = jnp.where(takes_far(offset), 0, mark(offset, 0))
        return begin * BLOCK, mark(offset, parts[2]) - begin

    def fourth(offset):
        begin = jnp.where(takes_far(offset), far_middle(offset), far_begin(offset))
        return begin * BLOCK, blocks - begin

    def last(offset):
        begin = mark(offset, parts[2])
        last_row = jnp.minimum((2 * seg + 35 - offset) // 8 * 8, window)
        return begin * BLOCK, (last_row - begin * BLOCK + BLOCK - 1) // BLOCK

    def near_pieces(k, arrays, halo, begin=None):
        return part_pieces(k, arrays, halo, 1, begin, None, 1) + part_pieces(k, arrays + 1, halo + 1, 1, begin, None, 0)

    own_pieces = pieces_of(0, 1, 0, 0, seg)
    top_piece = (None, 2, None, 0, ROWHALO, QUARTERS - 1, -ROWHALO)
    out = phase(
        None, [record, own[0], top, far[0], far[1]], [],
        [top_piece] + own_pieces + part_pieces(0, 3, 3, 2) + part_pieces(1, 4, 3, 2), second,
    )
    out = phase(
        out, [record, own[0], top, passed[0], given[0], passed[1], given[1]], [],
        [top_piece] + own_pieces + near_pieces(0, 3, 3) + near_pieces(1, 5, 3), third,
    )
    out = phase(
        out, [far[0], far[1], far[2], far[3], bot], [],
        [piece for k in range(4) for piece in part_pieces(k, k, 0, 2)]
        + [(None, 4, None, 0, ROWHALO, 0, 3 * seg)], fourth,
    )
    return phase(
        out, [passed[0], given[0], passed[1], given[1], passed[2], given[2], passed[3], given[3], far[0], far[1]], [],
        near_pieces(1, 2, 0, parts[2] - 128) + near_pieces(2, 4, 0) + near_pieces(3, 6, 0)
        + part_pieces(0, 8, 8, 2) + part_pieces(1, 9, 8, 2, end=q),
        last,
    )


def solution(mesh):
    return jax.shard_map(
        on_device,
        mesh=mesh,
        in_specs=(P("shot", "rcv"), P("shot"), P("shot"), P()),
        out_specs=P("shot", None, "rcv"),
        check_vma=False,
    )
```

time: 439 us -> 141 us (0.32)
  the two profiles are of different devices: /device:TPU:9 before, /device:TPU:13 now
where the time goes in v2:
time: 141 us; the launch traced here: 140 us
  Pallas kernels  66.3 us (47%)
  starting transfers between devices  42.6 us (30%)
  waiting for transfers between devices  27.1 us (19%)
  between operations  1.8 us (1%)
    pallas_call x4, Pallas kernels, phase(): pl.pallas_call(functools.partial(deblend_kernel, (seg, columns, len(array...  61.4 us
    ppermute x9, waiting for transfers between devices, shifted(): return lax.ppermute(shard, axis, pairs)  27 us
    ppermute x9, starting transfers between devices, shifted(): return lax.ppermute(shard, axis, pairs)  24.6 us
    ppermute x4, starting transfers between devices, on_device(): given = [lax.ppermute(x, 'shot', to_even) for x in own]  12.9 us
    ppermute x4, starting transfers between devices, on_device(): passed = [lax.ppermute(x, 'shot', to_odd) for x in far]  5.15 us
  transfers between devices with their start and end apart: 17, of which 5 were waited for; matrix products, arithmetic and copies ran while one was open for 1% of the time, Pallas kernels for 30%

profile of v2, /device:TPU:13, one launch (start us, length us, event | category | flops | bytes accessed | tf_op | source)
XLA Modules:
  0.0 139.8 jit_solution(3760201867223953895)
XLA Ops:
  0.0 2.1 %shard_map.64 = (f32[256,128]{1,0:T(8,128)}, f32[256,128]{1,0:T(8,128)}) custom-call(bf16[1024,512]{1,0:T(8,128)(2,1)} %refs_0_.3), custom_call_target="tpu_custom_call" | custom-call | tf_op jit(solution)/shard_map/pallas_call | solution.py:347
  2.1 3.7 %collective-permute-start.1 = (f32[256,128]{1,0:T(8,128)}, f32[256,128]{1,0:T(8,128)S(1)}, u32[]{:S(2)}, u32[]{:S(2)}) collective-permute-start(f32[256,128]{1,0:T(8,128)} %get-tuple-element.13), channel_id=1, source_target_pairs={{0,1},{1,2},{2,3},{4,5},{5,6},{6,7},{8,9},{9,10},{10,11},{12,13},{... | collective-permute-start | bytes 393224 | tf_op jit(solution)/shard_map/ppermute | solution.py:29
  5.7 1.9 %collective-permute-start.2 = (f32[256,128]{1,0:T(8,128)}, f32[256,128]{1,0:T(8,128)S(1)}, u32[]{:S(2)}, u32[]{:S(2)}) collective-permute-start(f32[256,128]{1,0:T(8,128)} %get-tuple-element.14), channel_id=1, source_target_pairs={{1,0},{2,1},{3,2},{5,4},{6,5},{7,6},{9,8},{10,9},{11,10},{13,12},{... | collective-permute-start | bytes 393224 | tf_op jit(solution)/shard_map/ppermute | solution.py:29
  9.0 3.3 %collective-permute-done.2.right = f32[256,128]{1,0:T(8,128)S(1)} collective-permute-done((f32[256,128]{1,0:T(8,128)}, f32[256,128]{1,0:T(8,128)S(1)}, u32[]{:S(2)}, u32[]{:S(2)}) %collective-permute-start.2) | collective-permute-done | bytes 131104 | tf_op jit(solution)/shard_map/ppermute | solution.py:29
  12.2 0.6 copy-done.8
  12.9 2.8 %shard_map.65 = (f32[16,768]{1,0:T(8,128)}, f32[24,768]{1,0:T(8,128)}, f32[248,512]{1,0:T(8,128)}, f32[304,512]{1,0:T(8,128)}, f32[304,512]{1,0:T(8,128)}, /*index=5*/f32[304,512]{1,0:T(8,128)}) custom-call(s32[1]{0:T(128)} %copy.18.offsets, s32[1]{0:T(128)} %copy.19.lengths, bf16[1024,512]{1,0:T(8,128)(2,1)} %refs_0_.3, f32[256,128]{1,0:T(8,128)} %copy-done.7, ...), custom_call_target="tpu_custom_call" | custom-call | tf_op jit(solution)/shard_map/pallas_call | solution.py:354
  15.7 2.1 %collective-permute-start.4 = (f32[248,512]{1,0:T(8,128)}, f32[248,512]{1,0:T(8,128)S(1)}, u32[]{:S(2)}, u32[]{:S(2)}) collective-permute-start(f32[248,512]{1,0:T(8,128)} %get-tuple-element.16.refs_1_), channel_id=1, source_target_pairs={{8,0},{12,4},{16,8},{20,12},{24,16},{28,20},{9,1},{13,5},{17,9},{2... | collective-permute-start | bytes 1523720 | tf_op jit(solution)/shard_map/ppermute | solution.py:29
  17.8 2.2 %collective-permute-start.6 = (f32[248,512]{1,0:T(8,128)}, f32[248,512]{1,0:T(8,128)S(1)}, u32[]{:S(2)}, u32[]{:S(2)}) collective-permute-start(f32[248,512]{1,0:T(8,128)} %get-tuple-element.16.refs_1_), channel_id=1, source_target_pairs={{4,0},{12,8},{20,16},{28,24},{5,1},{13,9},{21,17},{29,25},{6,2},{1... | collective-permute-start | bytes 1523720 | tf_op jit(solution)/shard_map/ppermute | solution.py:364
  19.9 1.9 %collective-permute-start.7 = (f32[304,512]{1,0:T(8,128)}, f32[304,512]{1,0:T(8,128)S(1)}, u32[]{:S(2)}, u32[]{:S(2)}) collective-permute-start(f32[304,512]{1,0:T(8,128)} %get-tuple-element.17), channel_id=1, source_target_pairs={{8,0},{12,4},{16,8},{20,12},{24,16},{28,20},{9,1},{13,5},{17,9},{2... | collective-permute-start | bytes 1867784 | tf_op jit(solution)/shard_map/ppermute | solution.py:29
  21.9 2.4 %collective-permute-start.3 = (f32[24,768]{1,0:T(8,128)}, f32[24,768]{1,0:T(8,128)S(1)}, u32[]{:S(2)}, u32[]{:S(2)}) collective-permute-start(f32[24,768]{1,0:T(8,128)} %get-tuple-element.15), channel_id=1, source_target_pairs={{0,4},{4,8},{8,12},{12,16},{16,20},{20,24},{24,28},{1,5},{5,9},{9,... | collective-permute-start | bytes 221192 | tf_op jit(solution)/shard_map/ppermute | solution.py:29
  24.3 0.1 add_convert_fusion
  24.4 3.2 %collective-permute-start = (f32[2]{0:T(128)S(1)}, f32[2]{0:T(128)S(1)}, u32[]{:S(2)}, u32[]{:S(2)}) collective-permute-start(f32[2]{0:T(128)S(1)} %add_convert_fusion), channel_id=1, source_target_pairs={{0,8},{4,12},{8,16},{12,20},{16,24},{20,28},{1,9},{5,13},{9,17},{1... | collective-permute-start | bytes 32 | tf_op jit(solution)/shard_map/ppermute | solution.py:29
  27.6 1.3 collective-permute-done
  29.0 2.9 %collective-permute-start.9 = (f32[304,512]{1,0:T(8,128)}, f32[304,512]{1,0:T(8,128)S(1)}, u32[]{:S(2)}, u32[]{:S(2)}) collective-permute-start(f32[304,512]{1,0:T(8,128)} %get-tuple-element.17), channel_id=1, source_target_pairs={{4,0},{12,8},{20,16},{28,24},{5,1},{13,9},{21,17},{29,25},{6,2},{1... | collective-permute-start | bytes 1867784 | tf_op jit(solution)/shard_map/ppermute | solution.py:364
  31.9 1.9 %collective-permute-start.10 = (f32[304,512]{1,0:T(8,128)}, f32[304,512]{1,0:T(8,128)}, u32[]{:S(2)}, u32[]{:S(2)}) collective-permute-start(f32[304,512]{1,0:T(8,128)} %get-tuple-element.18), channel_id=1, source_target_pairs={{8,0},{12,4},{16,8},{20,12},{24,16},{28,20},{9,1},{13,5},{17,9},{2... | collective-permute-start | bytes 1867784 | tf_op jit(solution)/shard_map/ppermute | solution.py:29
  33.8 1.9 %collective-permute-start.13 = (f32[304,512]{1,0:T(8,128)}, f32[304,512]{1,0:T(8,128)}, u32[]{:S(2)}, u32[]{:S(2)}) collective-permute-start(f32[304,512]{1,0:T(8,128)} %get-tuple-element.19), channel_id=1, source_target_pairs={{8,0},{12,4},{16,8},{20,12},{24,16},{28,20},{9,1},{13,5},{17,9},{2... | collective-permute-start | bytes 1867784 | tf_op jit(solution)/shard_map/ppermute | solution.py:29
  35.8 1.3 collective-permute-start.5
  37.1 7.8 %collective-permute-done.7.refs_4_.refs_1_.refs_9_ = f32[304,512]{1,0:T(8,128)S(1)} collective-permute-done((f32[304,512]{1,0:T(8,128)}, f32[304,512]{1,0:T(8,128)S(1)}, u32[]{:S(2)}, u32[]{:S(2)}) %collective-permute-start.7) | collective-permute-done | bytes 622624 | tf_op jit(solution)/shard_map/ppermute | solution.py:29
  44.9 1.3 collective-permute-start.8
  46.2 4.9 %collective-permute-start.12 = (f32[304,512]{1,0:T(8,128)}, f32[304,512]{1,0:T(8,128)}, u32[]{:S(2)}, u32[]{:S(2)}) collective-permute-start(f32[304,512]{1,0:T(8,128)} %get-tuple-element.18), channel_id=1, source_target_pairs={{4,0},{12,8},{20,16},{28,24},{5,1},{13,9},{21,17},{29,25},{6,2},{1... | collective-permute-start | bytes 1867784 | tf_op jit(solution)/shard_map/ppermute | solution.py:364
  51.1 7.2 %collective-permute-done.10.refs_2_ = f32[304,512]{1,0:T(8,128)} collective-permute-done((f32[304,512]{1,0:T(8,128)}, f32[304,512]{1,0:T(8,128)}, u32[]{:S(2)}, u32[]{:S(2)}) %collective-permute-start.10) | collective-permute-done | bytes 622624 | tf_op jit(solution)/shard_map/ppermute | solution.py:29
  58.2 3.0 %collective-permute-start.15 = (f32[304,512]{1,0:T(8,128)}, f32[304,512]{1,0:T(8,128)}, u32[]{:S(2)}, u32[]{:S(2)}) collective-permute-start(f32[304,512]{1,0:T(8,128)} %get-tuple-element.19), channel_id=1, source_target_pairs={{4,0},{12,8},{20,16},{28,24},{5,1},{13,9},{21,17},{29,25},{6,2},{1... | collective-permute-start | bytes 1867784 | tf_op jit(solution)/shard_map/ppermute | solution.py:364
  61.2 7.4 %collective-permute-done.13.refs_3_ = f32[304,512]{1,0:T(8,128)} collective-permute-done((f32[304,512]{1,0:T(8,128)}, f32[304,512]{1,0:T(8,128)}, u32[]{:S(2)}, u32[]{:S(2)}) %collective-permute-start.13) | collective-permute-done | bytes 622624 | tf_op jit(solution)/shard_map/ppermute | solution.py:29
  68.6 1.3 collective-permute-start.11
  70.0 1.3 collective-permute-start.14
  71.3 5.5 %collective-permute-start.16 = (f32[16,768]{1,0:T(8,128)}, f32[16,768]{1,0:T(8,128)S(1)}, u32[]{:S(2)}, u32[]{:S(2)}) collective-permute-start(f32[16,768]{1,0:T(8,128)} %get-tuple-element.20), channel_id=1, source_target_pairs={{12,0},{16,4},{20,8},{24,12},{28,16},{13,1},{17,5},{21,9},{25,13},... | collective-permute-start | bytes 147464 | tf_op jit(solution)/shard_map/ppermute | solution.py:29
  76.9 0.6 convert_element_type.17.params
  77.5 11.6 %shard_map.66.refs_7_ = f32[1,2048,512]{2,1,0:T(8,128)} custom-call(s32[5,2]{1,0:T(8,128)} %convert_element_type.17.params, f32[3]{0:T(128)} %thr.7, bf16[768,640]{1,0:T(8,128)(2,1)} %constant.4.clone.into, bf16[640,512]{1,0:T(8,128)(2,1)} %constant.5.clone.back, bf16[1024,512]{1,0:T(8,128)(2,1)} %refs_0_.3, f32[248,512]{1,0:T(8,128)} %get-tuple-element.16.refs_1_, ...), custom_call_target="tpu_custom_call" | custom-call | tf_op jit(solution)/shard_map/pallas_call | solution.py:377
  89.2 13.3 %shard_map.67.refs_5_ = f32[1,2048,512]{2,1,0:T(8,128)} custom-call(s32[5,2]{1,0:T(8,128)} %convert_element_type.17.params, f32[3]{0:T(128)} %thr.7, bf16[768,640]{1,0:T(8,128)(2,1)} %constant.4.clone.into, bf16[640,512]{1,0:T(8,128)(2,1)} %constant.5.clone.back, bf16[1024,512]{1,0:T(8,128)(2,1)} %refs_0_.3, ...), custom_call_target="tpu_custom_call", output_to_operand_aliasing={{}: (11, {})} | custom-call | tf_op jit(solution)/shard_map/pallas_call | solution.py:377
  102.5 0.6 copy-done.9
  103.1 17.6 %shard_map.68.refs_10_ = f32[1,2048,512]{2,1,0:T(8,128)} custom-call(s32[5,2]{1,0:T(8,128)} %convert_element_type.17.params, f32[3]{0:T(128)} %thr.7, bf16[768,640]{1,0:T(8,128)(2,1)} %constant.4.clone.into, bf16[640,512]{1,0:T(8,128)(2,1)} %constant.5.clone.back, f32[248,512]{1,0:T(8,128)} %copy-done.1, ...), custom_call_target="tpu_custom_call", output_to_operand_aliasing={{}: (9, {})} | custom-call | tf_op jit(solution)/shard_map/pallas_call | solution.py:377
  120.7 18.9 %shard_map.69 = f32[1,2048,512]{2,1,0:T(8,128)} custom-call(s32[5,2]{1,0:T(8,128)} %convert_element_type.17.params, f32[3]{0:T(128)} %thr.7, bf16[768,640]{1,0:T(8,128)(2,1)} %constant.4.clone.into, bf16[640,512]{1,0:T(8,128)(2,1)} %constant.5.clone.back, f32[248,512]{1,0:T(8,128)} %copy-done.5, ...), custom_call_target="tpu_custom_call", output_to_operand_aliasing={{}: (14, {})} | custom-call | tf_op jit(solution)/shard_map/pallas_call | solution.py:377
  (35 shorter events, 0.2 us)
Async XLA Ops:
  2.1 6.9 %collective-permute-start.1 = (f32[256,128]{1,0:T(8,128)}, f32[256,128]{1,0:T(8,128)S(1)}, u32[]{:S(2)}, u32[]{:S(2)}) collective-permute-start(f32[256,128]{1,0:T(8,128)} %get-tuple-element.13), channel_id=1, source_target_pairs={{0,1},{1,2},{2,3},{4,5},{5,6},{6,7},{8,9},{9,10},{10,11},{12,13},{... | collective-permute-start | bytes 393224 | tf_op jit(solution)/shard_map/ppermute | solution.py:29
  5.7 6.5 %collective-permute-start.2 = (f32[256,128]{1,0:T(8,128)}, f32[256,128]{1,0:T(8,128)S(1)}, u32[]{:S(2)}, u32[]{:S(2)}) collective-permute-start(f32[256,128]{1,0:T(8,128)} %get-tuple-element.14), channel_id=1, source_target_pairs={{1,0},{2,1},{3,2},{5,4},{6,5},{7,6},{9,8},{10,9},{11,10},{13,12},{... | collective-permute-start | bytes 393224 | tf_op jit(solution)/shard_map/ppermute | solution.py:29
  9.0 3.3 %copy-start.7 = (f32[256,128]{1,0:T(8,128)}, f32[256,128]{1,0:T(8,128)S(1)}, u32[]{:S(2)}) copy-start(f32[256,128]{1,0:T(8,128)S(1)} %collective-permute-done.1.left) | copy-start | bytes 393220
  12.2 0.6 copy-start.8
  15.7 18.1 %collective-permute-start.4 = (f32[248,512]{1,0:T(8,128)}, f32[248,512]{1,0:T(8,128)S(1)}, u32[]{:S(2)}, u32[]{:S(2)}) collective-permute-start(f32[248,512]{1,0:T(8,128)} %get-tuple-element.16.refs_1_), channel_id=1, source_target_pairs={{8,0},{12,4},{16,8},{20,12},{24,16},{28,20},{9,1},{13,5},{17,9},{2... | collective-permute-start | bytes 1523720 | tf_op jit(solution)/shard_map/ppermute | solution.py:29
  17.8 18.0 %collective-permute-start.6 = (f32[248,512]{1,0:T(8,128)}, f32[248,512]{1,0:T(8,128)S(1)}, u32[]{:S(2)}, u32[]{:S(2)}) collective-permute-start(f32[248,512]{1,0:T(8,128)} %get-tuple-element.16.refs_1_), channel_id=1, source_target_pairs={{4,0},{12,8},{20,16},{28,24},{5,1},{13,9},{21,17},{29,25},{6,2},{1... | collective-permute-start | bytes 1523720 | tf_op jit(solution)/shard_map/ppermute | solution.py:364
  19.9 24.9 %collective-permute-start.7 = (f32[304,512]{1,0:T(8,128)}, f32[304,512]{1,0:T(8,128)S(1)}, u32[]{:S(2)}, u32[]{:S(2)}) collective-permute-start(f32[304,512]{1,0:T(8,128)} %get-tuple-element.17), channel_id=1, source_target_pairs={{8,0},{12,4},{16,8},{20,12},{24,16},{28,20},{9,1},{13,5},{17,9},{2... | collective-permute-start | bytes 1867784 | tf_op jit(solution)/shard_map/ppermute | solution.py:29
  21.9 10.0 %collective-permute-start.3 = (f32[24,768]{1,0:T(8,128)}, f32[24,768]{1,0:T(8,128)S(1)}, u32[]{:S(2)}, u32[]{:S(2)}) collective-permute-start(f32[24,768]{1,0:T(8,128)} %get-tuple-element.15), channel_id=1, source_target_pairs={{0,4},{4,8},{8,12},{12,16},{16,20},{20,24},{24,28},{1,5},{5,9},{9,... | collective-permute-start | bytes 221192 | tf_op jit(solution)/shard_map/ppermute | solution.py:29
  24.4 4.6 %collective-permute-start = (f32[2]{0:T(128)S(1)}, f32[2]{0:T(128)S(1)}, u32[]{:S(2)}, u32[]{:S(2)}) collective-permute-start(f32[2]{0:T(128)S(1)} %add_convert_fusion), channel_id=1, source_target_pairs={{0,8},{4,12},{8,16},{12,20},{16,24},{20,28},{1,9},{5,13},{9,17},{1... | collective-permute-start | bytes 32 | tf_op jit(solution)/shard_map/ppermute | solution.py:29
  29.0 17.2 %collective-permute-start.9 = (f32[304,512]{1,0:T(8,128)}, f32[304,512]{1,0:T(8,128)S(1)}, u32[]{:S(2)}, u32[]{:S(2)}) collective-permute-start(f32[304,512]{1,0:T(8,128)} %get-tuple-element.17), channel_id=1, source_target_pairs={{4,0},{12,8},{20,16},{28,24},{5,1},{13,9},{21,17},{29,25},{6,2},{1... | collective-permute-start | bytes 1867784 | tf_op jit(solution)/shard_map/ppermute | solution.py:364
  31.8 45.6 %copy-start.6 = (f32[24,768]{1,0:T(8,128)}, f32[24,768]{1,0:T(8,128)S(1)}, u32[]{:S(2)}) copy-start(f32[24,768]{1,0:T(8,128)S(1)} %collective-permute-done.3.refs_2_) | copy-start | bytes 221188
  31.9 26.4 %collective-permute-start.10 = (f32[304,512]{1,0:T(8,128)}, f32[304,512]{1,0:T(8,128)}, u32[]{:S(2)}, u32[]{:S(2)}) collective-permute-start(f32[304,512]{1,0:T(8,128)} %get-tuple-element.18), channel_id=1, source_target_pairs={{8,0},{12,4},{16,8},{20,12},{24,16},{28,20},{9,1},{13,5},{17,9},{2... | collective-permute-start | bytes 1867784 | tf_op jit(solution)/shard_map/ppermute | solution.py:29
  33.8 43.7 %copy-start.1 = (f32[248,512]{1,0:T(8,128)}, f32[248,512]{1,0:T(8,128)S(1)}, u32[]{:S(2)}) copy-start(f32[248,512]{1,0:T(8,128)S(1)} %collective-permute-done.4.refs_3_.refs_0_.refs_8_) | copy-start | bytes 1523716
  33.8 34.8 %collective-permute-start.13 = (f32[304,512]{1,0:T(8,128)}, f32[304,512]{1,0:T(8,128)}, u32[]{:S(2)}, u32[]{:S(2)}) collective-permute-start(f32[304,512]{1,0:T(8,128)} %get-tuple-element.19), channel_id=1, source_target_pairs={{8,0},{12,4},{16,8},{20,12},{24,16},{28,20},{9,1},{13,5},{17,9},{2... | collective-permute-start | bytes 1867784 | tf_op jit(solution)/shard_map/ppermute | solution.py:29
  35.7 53.4 %copy-start.4 = (f32[248,512]{1,0:T(8,128)}, f32[248,512]{1,0:T(8,128)S(1)}, u32[]{:S(2)}) copy-start(f32[248,512]{1,0:T(8,128)S(1)} %collective-permute-done.6.refs_4_.refs_1_) | copy-start | bytes 1523716
  35.8 34.2 %collective-permute-start.5 = (f32[248,512]{1,0:T(8,128)S(1)}, f32[248,512]{1,0:T(8,128)S(1)}, u32[]{:S(2)}, u32[]{:S(2)}) collective-permute-start(f32[248,512]{1,0:T(8,128)S(1)} %collective-permute-done.4.refs_3_.refs_0_.refs_8_), channel_id=1, source_target_pairs={{0,4},{8,12},{16,20},{24,28},{1,5},{9,13},{17,21},{25,29},{2,6},{1... | collective-permute-start | bytes 1523720 | tf_op jit(solution)/shard_map/ppermute | solution.py:363
  44.9 32.6 %copy-start = (f32[304,512]{1,0:T(8,128)}, f32[304,512]{1,0:T(8,128)S(1)}, u32[]{:S(2)}) copy-start(f32[304,512]{1,0:T(8,128)S(1)} %collective-permute-done.7.refs_4_.refs_1_.refs_9_) | copy-start | bytes 1867780
  44.9 26.4 %collective-permute-start.8 = (f32[304,512]{1,0:T(8,128)S(1)}, f32[304,512]{1,0:T(8,128)S(1)}, u32[]{:S(2)}, u32[]{:S(2)}) collective-permute-start(f32[304,512]{1,0:T(8,128)S(1)} %collective-permute-done.7.refs_4_.refs_1_.refs_9_), channel_id=1, source_target_pairs={{0,4},{8,12},{16,20},{24,28},{1,5},{9,13},{17,21},{25,29},{2,6},{1... | collective-permute-start | bytes 1867784 | tf_op jit(solution)/shard_map/ppermute | solution.py:363
  46.2 42.9 %copy-start.2 = (f32[304,512]{1,0:T(8,128)}, f32[304,512]{1,0:T(8,128)S(1)}, u32[]{:S(2)}) copy-start(f32[304,512]{1,0:T(8,128)S(1)} %collective-permute-done.9.refs_6_.refs_3_) | copy-start | bytes 1867780
  46.2 74.5 %collective-permute-start.12 = (f32[304,512]{1,0:T(8,128)}, f32[304,512]{1,0:T(8,128)}, u32[]{:S(2)}, u32[]{:S(2)}) collective-permute-start(f32[304,512]{1,0:T(8,128)} %get-tuple-element.18), channel_id=1, source_target_pairs={{4,0},{12,8},{20,16},{28,24},{5,1},{13,9},{21,17},{29,25},{6,2},{1... | collective-permute-start | bytes 1867784 | tf_op jit(solution)/shard_map/ppermute | solution.py:364
  58.2 62.5 %collective-permute-start.15 = (f32[304,512]{1,0:T(8,128)}, f32[304,512]{1,0:T(8,128)}, u32[]{:S(2)}, u32[]{:S(2)}) collective-permute-start(f32[304,512]{1,0:T(8,128)} %get-tuple-element.19), channel_id=1, source_target_pairs={{4,0},{12,8},{20,16},{28,24},{5,1},{13,9},{21,17},{29,25},{6,2},{1... | collective-permute-start | bytes 1867784 | tf_op jit(solution)/shard_map/ppermute | solution.py:364
  68.6 52.1 %collective-permute-start.11 = (f32[304,512]{1,0:T(8,128)}, f32[304,512]{1,0:T(8,128)}, u32[]{:S(2)}, u32[]{:S(2)}) collective-permute-start(f32[304,512]{1,0:T(8,128)} %collective-permute-done.10.refs_2_), channel_id=1, source_target_pairs={{0,4},{8,12},{16,20},{24,28},{1,5},{9,13},{17,21},{25,29},{2,6},{1... | collective-permute-start | bytes 1867784 | tf_op jit(solution)/shard_map/ppermute | solution.py:363
  69.9 19.2 %copy-start.5 = (f32[248,512]{1,0:T(8,128)}, f32[248,512]{1,0:T(8,128)S(1)}, u32[]{:S(2)}) copy-start(f32[248,512]{1,0:T(8,128)S(1)} %collective-permute-done.5.refs_3_.refs_0_) | copy-start | bytes 1523716
  70.0 50.8 %collective-permute-start.14 = (f32[304,512]{1,0:T(8,128)}, f32[304,512]{1,0:T(8,128)}, u32[]{:S(2)}, u32[]{:S(2)}) collective-permute-start(f32[304,512]{1,0:T(8,128)} %collective-permute-done.13.refs_3_), channel_id=1, source_target_pairs={{0,4},{8,12},{16,20},{24,28},{1,5},{9,13},{17,21},{25,29},{2,6},{1... | collective-permute-start | bytes 1867784 | tf_op jit(solution)/shard_map/ppermute | solution.py:363
  71.3 17.8 %copy-start.3 = (f32[304,512]{1,0:T(8,128)}, f32[304,512]{1,0:T(8,128)S(1)}, u32[]{:S(2)}) copy-start(f32[304,512]{1,0:T(8,128)S(1)} %collective-permute-done.8.refs_5_.refs_2_) | copy-start | bytes 1867780
  71.3 31.1 %collective-permute-start.16 = (f32[16,768]{1,0:T(8,128)}, f32[16,768]{1,0:T(8,128)S(1)}, u32[]{:S(2)}, u32[]{:S(2)}) collective-permute-start(f32[16,768]{1,0:T(8,128)} %get-tuple-element.20), channel_id=1, source_target_pairs={{12,0},{16,4},{20,8},{24,12},{28,16},{13,1},{17,5},{21,9},{25,13},... | collective-permute-start | bytes 147464 | tf_op jit(solution)/shard_map/ppermute | solution.py:29
  102.5 0.6 copy-start.9

commit v3 on v2

v3 whole, which is shorter than its diff:
```python
import functools

import numpy as np
import jax
import jax.numpy as jnp
from jax import lax
from jax.experimental import pallas as pl
from jax.experimental.pallas import tpu as pltpu
from jax.sharding import PartitionSpec as P

LEVELS = 3
relax_step = 0.5

PLANES = 5
LANES = 128
RING = PLANES * LANES
EDGE = 32
QUARTERS = LANES // EDGE
HEAD = 128
PAD = 64
ROWHALO = 16
BLOCK = 64
STRIP = 64


def shifted(shard, axis, by):
    devices = lax.axis_size(axis)
    pairs = [(i, i + by) for i in range(devices) if 0 <= i + by < devices]
    return lax.ppermute(shard, axis, pairs)


def ring_matrices(columns):
    wide = columns + 2 * LANES
    into = np.zeros((wide, RING), np.float32)
    back = np.zeros((RING, columns), np.float32)

    def place(ring):
        return (ring % PLANES) * LANES + ring // PLANES

    for column in range(columns):
        into[column, place(column)] = relax_step
        back[place(column), column] = 1.0
    for quarter in range(LANES // EDGE):
        for i in range(EDGE):
            into[columns + quarter * EDGE + i, place(RING - EDGE + i)] = relax_step
            into[columns + LANES + quarter * EDGE + i, place(columns + i)] = relax_step
    return jnp.asarray(into, jnp.bfloat16), jnp.asarray(back, jnp.bfloat16)


def smooth_across(planes, dilation):
    rolled = {}

    def at(position):
        turns, plane = divmod(position, PLANES)
        if turns == 0:
            return planes[plane]
        if (turns, plane) not in rolled:
            rolled[turns, plane] = pltpu.roll(planes[plane], (-turns) % LANES, 1)
        return rolled[turns, plane]

    return [
        (at(k - 2 * dilation) + at(k + 2 * dilation))
        + 4.0 * (at(k - dilation) + at(k + dilation))
        + 6.0 * planes[k]
        for k in range(PLANES)
    ]


def limit(values, cut):
    return jnp.minimum(jnp.maximum(values, -cut), cut)


def pairs_of(first, count, body):
    def step(b, carry):
        body(pl.multiple_of(first + b * (2 * BLOCK), 8))
        return carry

    lax.fori_loop(0, (count + 1) // 2, step, 0)


def smooth_block(ref, start, rows, dilation, scale):
    centre, summed = [], []
    for k in range(PLANES):
        x = [ref[k, pl.ds(start + tap * dilation, rows), :] for tap in range(-2, 3)]
        centre.append(x[2])
        summed.append((x[0] + x[4]) + 4.0 * (x[1] + x[3]) + 6.0 * x[2])
    summed = smooth_across(summed, dilation)
    return centre, [s * w for s, w in zip(summed, scale)]


def deblend_kernel(geometry, pieces, halo_places, outer, span, operands, params, thr, *refs):
    seg, columns = geometry
    into_hbm, back_hbm, *sources = refs[:operands]
    out, into, back, ext, halos, beyond, gathered, c1, c2, f, strip, staged, sem, out_sem = refs[operands:]
    window = 2 * seg
    quarter_rows = seg // QUARTERS
    pair = 2 * BLOCK

    shots = lax.axis_size("shot")
    me = lax.axis_index("shot")
    rcv = lax.axis_index("rcv")
    offset = params[2, 0]
    live = params[2, 1]
    total = (shots - me) * seg - offset

    def shot(by):
        return by * seg + params[by + 2, 0] - offset, params[by + 2, 1]

    spans = [(pl.multiple_of(begin * BLOCK, 8), jnp.maximum(end - begin, 0)) for begin, end in span(offset)]
    some = sum(count for _, count in spans) > 0

    def reached(row, rows):
        found = False
        for low, count in spans:
            inside = (row < offset + low + count * BLOCK + 40) & (row + rows > offset + low - 40)
            found = found | ((count > 0) & inside)
        return found

    def copy_of(n, src, target):
        return pltpu.make_async_copy(src, target, sem.at[n])

    brought = [(0, None, into, some)]
    for main, first, rows, row in pieces:
        brought.append((main, (first, rows), ext.at[pl.ds(row, rows), :], reached(row, rows)))
    for segment, place in enumerate(halo_places):
        if place is not None:
            brought.append((place, (0, HEAD), halos.at[segment], some))
    if outer is not None:
        brought.append((outer[0], (0, ROWHALO), beyond, reached(outer[1], ROWHALO)))

    pl.when(some)(lambda: copy_of(0, into_hbm, into).start())
    for n, (place, part, target, wanted) in enumerate(brought):
        if part is not None:
            pl.when(wanted)(lambda: copy_of(n, sources[place].at[pl.ds(*part), :], target).start())
    pl.when(some)(lambda: copy_of(len(brought), back_hbm, back).start())

    lane = lax.broadcasted_iota(jnp.int32, (1, LANES), 1)
    has_right = jnp.where(rcv < lax.axis_size("rcv") - 1, 1.0, 0.0)
    has_left = jnp.where(rcv > 0, 1.0, 0.0)
    scale = []
    for k in range(PLANES):
        ring = lane * PLANES + k
        side = jnp.where(ring < columns + LANES // 2, has_right, has_left)
        scale.append(jnp.where(ring < columns, 1.0, side) * (1.0 / 256.0))
    strip[:, :, 0:16, :] = jnp.zeros((3, PLANES, 16, LANES), jnp.float32)
    strip[:, :, 16 + STRIP : 32 + STRIP, :] = jnp.zeros((3, PLANES, 16, LANES), jnp.float32)

    for n, (place, part, target, wanted) in enumerate(brought):
        pl.when(wanted)(lambda: copy_of(n, target, target).wait())

    def permute_in(main, left, right, quarter, row):
        mine = (lane // EDGE) == quarter
        lhs = [main] + [jnp.where(mine, x, 0.0) for x in (left, right)]
        lhs = jnp.concatenate([x.astype(jnp.bfloat16) for x in lhs], axis=1)
        result = jnp.dot(lhs, into[...], preferred_element_type=jnp.float32)
        for k in range(PLANES):
            gathered[0, k, pl.ds(PAD + row, main.shape[0]), :] = result[:, k * LANES : (k + 1) * LANES]

    def permute_quarter(i, carry):
        row = pl.multiple_of(i * quarter_rows, quarter_rows)
        segment = row // seg
        sides = []
        for side in range(2):
            lanes = [2 * side * LANES + at // HEAD * LANES for at in range(0, quarter_rows, HEAD)]
            sides.append(jnp.concatenate([halos[segment, :, at : at + LANES] for at in lanes], axis=0))
        permute_in(ext[pl.ds(row, quarter_rows), :], *sides, lax.rem(row, seg) // quarter_rows, row)
        return carry

    for low, count in spans:
        begin = jnp.clip((offset + low - 40) // quarter_rows, 0, 3 * QUARTERS)
        end = jnp.clip((offset + low + count * BLOCK + 40 + quarter_rows - 1) // quarter_rows, 0, 3 * QUARTERS)
        lax.fori_loop(begin, jnp.where(count > 0, end, begin), permute_quarter, 0)
    if outer is not None:

        @pl.when(reached(outer[1], ROWHALO))
        def _():
            quarter = QUARTERS - 1 if outer[1] < 0 else 0
            sides = [beyond[:, columns + side * LANES : columns + (side + 1) * LANES] for side in range(2)]
            permute_in(beyond[:, 0:columns], *sides, quarter, outer[1])

    def level_pass(source, shift, target, dilation, first, count):
        def body(at):
            _, summed = smooth_block(source, at + shift, pair, dilation, scale)
            for k in range(PLANES):
                target[k, pl.ds(at, pair), :] = summed[k]

        pairs_of(first, count, body)

    def shrunk(sweep, shift, at):
        centre, summed = smooth_block(c2, at, pair, 4, scale)
        for k in range(PLANES):
            x0 = gathered[sweep, k, pl.ds(at + shift, pair), :]
            x1 = c1[k, pl.ds(at, pair), :]
            x2 = centre[k]
            clipped = limit(x0 - x1, thr[0]) + limit(x1 - x2, thr[1]) + limit(x2 - summed[k], thr[2])
            yield k, x0, x0 - clipped

    def next_gathered(at):
        t = at - PAD + lax.broadcasted_iota(jnp.int32, (pair, LANES), 0)
        shots_live = jnp.zeros(t.shape, jnp.float32)
        for by in range(-2, 3):
            begin, length = shot(by)
            shots_live = shots_live + jnp.where((t >= begin) & (t < begin + length), 1.0, 0.0)
        own_live = jnp.where((t >= 0) & (t < live), 1.0, 0.0)
        inside = jnp.where(t < total, relax_step, 0.0)
        factor = own_live * (1.0 - inside * shots_live)
        for k, x0, value in shrunk(0, offset, at):
            f[k, pl.ds(at, pair), :] = value
            gathered[1, k, pl.ds(at, pair), :] = own_live * x0 + factor * value

    half = STRIP // 2

    def do_strip(by, at_end):
        begin, length = shot(by)
        p = begin + jnp.where(at_end, length, 0)
        t = p - half + lax.broadcasted_iota(jnp.int32, (STRIP, LANES), 0)
        in_live = jnp.where((t >= begin) & (t < begin + length), 1.0, 0.0)
        in_window = jnp.where((t >= begin) & (t < begin + window), 1.0, 0.0)
        for k in range(PLANES):
            strip[0, k, 16 : 16 + STRIP, :] = gathered[0, k, pl.ds(PAD + offset + p - half, STRIP), :] * in_live
        for j in range(2):
            _, summed = smooth_block(strip.at[j], 16, STRIP, 2**j, scale)
            for k in range(PLANES):
                strip[j + 1, k, 16 : 16 + STRIP, :] = summed[k] * in_window
        mid = half
        _, summed = smooth_block(strip.at[2], mid, 32, 4, scale)
        t = p - 16 + lax.broadcasted_iota(jnp.int32, (32, LANES), 0)
        in_window = jnp.where((t >= begin) & (t < begin + window), 1.0, 0.0)
        near_edge = (t >= begin) & (t < begin + length) & (t >= p - 14) & (t < p + 14)
        own_live = (t >= 0) & (t < live)
        inside = jnp.where(t < total, -relax_step, 0.0)
        weight = jnp.where(near_edge & own_live, inside + jnp.where(by == 0, 1.0, 0.0), 0.0)
        for k in range(PLANES):
            x0 = strip[0, k, mid : mid + 32, :]
            x1 = strip[1, k, mid : mid + 32, :]
            x2 = strip[2, k, mid : mid + 32, :]
            x3 = summed[k] * in_window
            clipped = limit(x0 - x1, thr[0]) + limit(x1 - x2, thr[1]) + limit(x2 - x3, thr[2])
            where = pl.ds(PAD + p - 16, 32)
            gathered[1, k, where, :] = gathered[1, k, where, :] + weight * (x0 - clipped - f[k, where, :])

    def out_copy(low, i):
        rows = pl.ds(pl.multiple_of(low + i * BLOCK, 8), BLOCK)
        return pltpu.make_async_copy(staged.at[rows, :], out.at[0, rows, :], out_sem.at[i])

    def estimate(low, count, at):
        t = at - PAD + lax.broadcasted_iota(jnp.int32, (pair, LANES), 0)
        own_live = jnp.where(t < live, 1.0, 0.0)
        high, rest = [], []
        for k, _, value in shrunk(1, 0, at):
            x = own_live * value
            h = x.astype(jnp.bfloat16)
            high.append(h)
            rest.append((x - h.astype(jnp.float32)).astype(jnp.bfloat16))
        both = jnp.concatenate([jnp.concatenate(high, axis=1), jnp.concatenate(rest, axis=1)], axis=0)
        result = jnp.dot(both, back[...], preferred_element_type=jnp.float32)
        staged[pl.ds(pl.multiple_of(at - PAD, 8), pair), :] = result[:pair] + result[pair:]
        i = (at - PAD - low) // BLOCK
        out_copy(low, i).start()
        pl.when(i + 1 < count)(lambda: out_copy(low, i + 1).start())

    def clear_edges(ref):
        ref[:, PAD - 16 : PAD, :] = jnp.zeros((PLANES, 16, LANES), jnp.float32)
        ref[:, PAD + window : PAD + window + 16, :] = jnp.zeros((PLANES, 16, LANES), jnp.float32)

    def process(low, count):
        high = low + count * BLOCK
        first = PAD + low
        wider, many = first - BLOCK // 2, count + 1

        def strip_step(i, carry):
            by, at_end = i // 2 - 2, i % 2 == 1
            begin, length = shot(by)
            p = begin + jnp.where(at_end, length, 0)
            begins_at = jnp.where(at_end, p - 14, p)
            bottom = jnp.maximum(low - 14, 0)
            top = jnp.minimum(high + 14, live)

            @pl.when((length > 0) & (begins_at + 14 > bottom) & (begins_at < top))
            def _():
                do_strip(by, at_end)

            return carry

        level_pass(gathered.at[0], offset, c1, 1, wider, many)
        level_pass(c1, 0, c2, 2, wider, many)
        pairs_of(wider, many, next_gathered)
        lax.fori_loop(1, 10, strip_step, 0)
        clear_edges(gathered.at[1])
        level_pass(gathered.at[1], 0, c1, 1, wider, many)
        clear_edges(c1)
        level_pass(c1, 0, c2, 2, wider, many)
        clear_edges(c2)
        pairs_of(first, count, lambda at: estimate(low, count, at))

        def wait(i, carry):
            out_copy(low, i).wait()
            return carry

        lax.fori_loop(0, count, wait, 0)

    pl.when(some)(lambda: copy_of(len(brought), back, back).wait())

    def span_step(i, carry):
        low, count = spans[0]
        if len(spans) > 1:
            low, count = jnp.where(i == 0, low, spans[1][0]), jnp.where(i == 0, count, spans[1][1])
        pl.when(count > 0)(lambda: process(pl.multiple_of(low, 8), count))
        return carry

    lax.fori_loop(0, len(spans), span_step, 0)


def prepare_kernel(record, first_edge, last_edge):
    seg, columns = record.shape
    quarter = seg // QUARTERS
    lane = lax.broadcasted_iota(jnp.int32, (1, LANES), 1)
    for out, start, inner in ((first_edge, 0, 0), (last_edge, columns - LANES, LANES - EDGE)):
        packed = jnp.zeros((quarter, LANES), jnp.float32)
        for q in range(QUARTERS):
            rows = record[q * quarter : (q + 1) * quarter, start : start + LANES].astype(jnp.float32)
            turn = (q * EDGE - inner) % LANES
            packed = jnp.where(lane // EDGE == q, pltpu.roll(rows, turn, 1) if turn else rows, packed)
        out[...] = packed


def header_kernel(parts, offsets, lengths, record, left, right, wide_first, wide_last, *own):
    seg, columns = record.shape
    quarter = seg // QUARTERS
    lane = lax.broadcasted_iota(jnp.int32, (8, LANES), 1)
    about = jnp.where(lane == 0, offsets[0], jnp.where(lane == 1, lengths[0], 0)).astype(jnp.float32)
    first = own[0]
    for side, halo in enumerate((left, right)):
        for part in range(quarter // HEAD):
            at = (2 * side + part) * LANES
            first[0:HEAD, at : at + LANES] = halo[part * HEAD : (part + 1) * HEAD, :]
    first[HEAD : HEAD + 8, :] = jnp.concatenate([about] * (columns // LANES), axis=1)
    first[HEAD + 8 :, :] = record[0 : parts[1], :].astype(jnp.float32)
    for k in range(1, len(own)):
        own[k][...] = record[parts[k] : parts[k + 1], :].astype(jnp.float32)
    wide_first[:, 0:columns] = record[0:ROWHALO, :].astype(jnp.float32)
    wide_last[0:ROWHALO, 0:columns] = record[seg - ROWHALO : seg, :].astype(jnp.float32)
    for side, halo in enumerate((left, right)):
        at = columns + side * LANES
        wide_first[:, at : at + LANES] = halo[0:ROWHALO, :]
        wide_last[0:ROWHALO, at : at + LANES] = halo[quarter - ROWHALO : quarter, :]
    wide_last[ROWHALO:, :] = jnp.concatenate([about] * (columns // LANES + 2), axis=1)


def pass_on_kernel(unread, own, far, *refs):
    sent, sem = refs[unread], refs[-1]
    odd = lax.rem(lax.axis_index("shot"), 2) == 1
    pl.when(odd)(lambda: pltpu.make_async_copy(own, sent, sem).start())
    pl.when(jnp.logical_not(odd))(lambda: pltpu.make_async_copy(far, sent, sem).start())
    pltpu.make_async_copy(own, sent, sem).wait()


def shots_kernel(second_last, last, mine, following, second, out):
    lane = lax.broadcasted_iota(jnp.int32, (8, LANES), 1)
    row = lax.broadcasted_iota(jnp.int32, (8, LANES), 0)
    found = jnp.zeros((8, LANES), jnp.float32)
    for n, pair in enumerate((second_last, last, mine, following, second)):
        if n in (0, 2):
            value = jnp.where(lane == 0, pair[0], pair[1])
        else:
            value = pair[0:1, :]
        found = jnp.where(row == n, value, found)
    out[...] = found.astype(jnp.int32)


def on_device(record, offsets, lengths, thresholds):
    seg, columns = record.shape
    window = 2 * seg
    shots = lax.axis_size("shot")
    q = seg // QUARTERS
    skip = HEAD + 8
    step = (seg + skip + 4 * 16 - 1) // (4 * 16) * 16
    parts = [0] + [seg - k * step for k in (3, 2, 1, 0)]
    swap = [(i, i ^ 1) for i in range(shots) if i ^ 1 < shots]
    smem = pl.BlockSpec(memory_space=pltpu.SMEM)
    anywhere = pl.BlockSpec(memory_space=pl.ANY)
    vmem = pl.BlockSpec(memory_space=pltpu.VMEM)

    def array(*shape):
        return jax.ShapeDtypeStruct(shape, jnp.float32)

    def part(k):
        return array(parts[k + 1] - parts[k] + (skip if k == 0 else 0), columns)

    first_edge, last_edge = pl.pallas_call(
        prepare_kernel, out_shape=(array(q, LANES), array(q, LANES)), in_specs=[vmem], out_specs=(vmem, vmem)
    )(record)
    from_left = shifted(last_edge, "rcv", 1)
    from_right = shifted(first_edge, "rcv", -1)
    mine = jnp.concatenate([offsets, lengths]).astype(jnp.float32)
    wide = columns + 2 * LANES
    def after(x, *others):
        return pl.pallas_call(
            lambda *refs: None,
            out_shape=jax.ShapeDtypeStruct(x.shape, x.dtype),
            in_specs=[anywhere] * (1 + len(others)),
            out_specs=anywhere,
            input_output_aliases={0: 0},
        )(x, *others)

    wide_first, wide_last, *own = pl.pallas_call(
        functools.partial(header_kernel, parts),
        out_shape=(array(ROWHALO, wide), array(ROWHALO + 8, wide)) + tuple(part(k) for k in range(4)),
        in_specs=[smem, smem, vmem, vmem, vmem],
        out_specs=(vmem,) * 6,
    )(offsets, lengths, record, from_left, from_right)
    swap = [(i, i ^ 1) for i in range(shots) if i ^ 1 < shots]
    far, near = [None] * 4, [None] * 4
    second_last = shifted(mine, "shot", 2)
    top = shifted(wide_last, "shot", 1)
    bot = shifted(wide_first, "shot", -3)
    far[0] = shifted(own[0], "shot", -2)
    own[1] = after(own[1], top)
    far[1] = shifted(own[1], "shot", -2)

    def pass_on(k, *others):
        ahead = [own[k + 2]] if k + 2 < 4 else []
        sent, *ahead = pl.pallas_call(
            functools.partial(pass_on_kernel, len(ahead) + len(others)),
            out_shape=(part(k),) + tuple(array(*x.shape) for x in ahead),
            in_specs=[anywhere] * (2 + len(ahead) + len(others)),
            out_specs=(vmem,) + (anywhere,) * len(ahead),
            input_output_aliases={2: 1} if ahead else {},
            scratch_shapes=[pltpu.SemaphoreType.DMA],
        )(own[k], far[k], *ahead, *others)
        near[k] = lax.ppermute(sent, "shot", swap)
        if ahead:
            own[k + 2] = ahead[0]
            far[k + 2] = shifted(own[k + 2], "shot", -2)

    pass_on(0)
    pass_on(1, near[0], second_last, bot)

    def corner(row):
        return pl.BlockSpec((8, LANES), lambda _: (row // 8, 0))

    params = pl.pallas_call(
        shots_kernel,
        grid=(1,),
        out_shape=jax.ShapeDtypeStruct((8, LANES), jnp.int32),
        in_specs=[smem, corner(ROWHALO), smem, corner(HEAD), corner(HEAD)],
        out_specs=vmem,
    )(second_last, top, mine, near[0], far[0])

    into, back = ring_matrices(columns)
    work = pltpu.VMEM((PLANES, window + 4 * PAD, LANES), jnp.float32)

    def phase(out, arrays, pieces, halo_places, outer, span):
        held = [] if out is None else [out]
        return pl.pallas_call(
            functools.partial(
                deblend_kernel, (seg, columns), pieces, halo_places, outer, span, 2 + len(arrays) + len(held)
            ),
            out_shape=array(1, window, columns),
            in_specs=[smem, smem] + [anywhere] * (2 + len(arrays) + len(held)),
            out_specs=anywhere,
            input_output_aliases={} if out is None else {4 + len(arrays): 0},
            scratch_shapes=[
                pltpu.VMEM(into.shape, into.dtype),
                pltpu.VMEM(back.shape, back.dtype),
                pltpu.VMEM((3 * seg, columns), jnp.float32),
                pltpu.VMEM((3, HEAD, columns), jnp.float32),
                pltpu.VMEM((ROWHALO, wide), jnp.float32),
                pltpu.VMEM((2, PLANES, 3 * seg + 4 * PAD, LANES), jnp.float32),
                work, work, work,
                pltpu.VMEM((3, PLANES, STRIP + 32, LANES), jnp.float32),
                pltpu.VMEM((window + BLOCK, columns), jnp.float32),
                pltpu.SemaphoreType.DMA((len(pieces) + 6,)),
                pltpu.SemaphoreType.DMA((window // BLOCK,)),
            ],
            compiler_params=pltpu.CompilerParams(vmem_limit_bytes=60 * 1024 * 1024),
        )(params, thresholds, into, back, *arrays, *held)

    def part_piece(k, main, segment):
        return (main, skip if k == 0 else 0, parts[k + 1] - parts[k], segment * seg + parts[k])

    blocks = window // BLOCK
    cap = 9

    def mark(offset, rows):
        return jnp.clip((seg + rows - 28 - offset) // BLOCK, 0, blocks)

    def far_begin(offset):
        return jnp.minimum((2 * seg + 35 - offset) // 8 * 8 // BLOCK, blocks)

    def far_middle(offset):
        return jnp.clip((2 * seg + parts[2] - 28 - offset) // BLOCK, far_begin(offset), blocks)

    def takes_far(offset):
        return far_middle(offset) - far_begin(offset) >= 4

    def first(offset):
        is_far = takes_far(offset)
        begin = jnp.where(is_far, far_begin(offset), 0)
        return [(begin, jnp.where(is_far, far_middle(offset), jnp.minimum(mark(offset, 0), cap)))]

    def second(offset):
        begin = jnp.where(takes_far(offset), 0, first(offset)[0][1])
        return [(begin, jnp.minimum(mark(offset, parts[2]), begin + cap))]

    def third(offset):
        is_far = takes_far(offset)
        return [(jnp.where(is_far, far_middle(offset), far_begin(offset)), blocks)]

    def last(offset):
        bridged = (jnp.minimum((2 * seg + 35 - offset) // 8 * 8, window) + BLOCK - 1) // BLOCK
        return [(second(offset)[0][1], bridged)]

    def every(places, segment):
        return [part_piece(k, place, segment) for k, place in enumerate(places)]

    own_pieces = every(range(4), 0)
    out = phase(None, [*own, top, far[0], far[1]], own_pieces + every((5, 6), 2), (0, None, 5), (4, -ROWHALO), first)
    pass_on(2, out, near[1])
    out = phase(
        out, [*own, top, near[0], near[1]], own_pieces + every((5, 6), 1), (0, 5, None), (4, -ROWHALO), second
    )
    pass_on(3, out, near[2])
    out = phase(out, [*far, bot], every(range(4), 2), (None, None, 0), (4, 3 * seg), third)
    return phase(
        out, [own[0], own[3], *near, far[0], far[1]],
        [part_piece(3, 1, 0)] + every(range(2, 6), 1) + every((6, 7), 2), (0, 2, 6), None, last,
    )


def solution(mesh):
    return jax.shard_map(
        on_device,
        mesh=mesh,
        in_specs=(P("shot", "rcv"), P("shot"), P("shot"), P()),
        out_specs=P("shot", None, "rcv"),
        check_vma=False,
    )
```

time: 141 us -> 130 us (0.922)
  the two profiles are of different devices: /device:TPU:13 before, /device:TPU:25 now
where the time goes in v3:
time: 130 us; the launch traced here: 128 us
  Pallas kernels  66 us (51%)
  starting transfers between devices  31.7 us (24%)
  waiting for transfers between devices  21.6 us (17%)
  local copies, waits for them, and re-layouts  7.11 us (5%)
  between operations  1.53 us (1%)
    pallas_call x4, Pallas kernels, phase(): pl.pallas_call(functools.partial(deblend_kernel, (seg, columns), pieces,...  52.1 us
    ppermute x9, starting transfers between devices, shifted(): return lax.ppermute(shard, axis, pairs)  25.3 us
    ppermute x4, waiting for transfers between devices, pass_on(): near[k] = lax.ppermute(sent, 'shot', swap)  14 us
    pallas_call x4, Pallas kernels, pass_on(): pl.pallas_call(functools.partial(pass_on_kernel, len(ahead) + len(others)...  7.63 us
    ppermute x9, waiting for transfers between devices, shifted(): return lax.ppermute(shard, axis, pairs)  7.61 us
    unnamed x28, local copies, waits for them, and re-layouts  7.11 us
    ppermute x4, starting transfers between devices, pass_on(): near[k] = lax.ppermute(sent, 'shot', swap)  6.41 us
    pallas_call x1, Pallas kernels, on_device(): pl.pallas_call(functools.partial(header_kernel, parts), out_shape=(array(...  2.8 us
  transfers between devices with their start and end apart: 13, of which 6 were waited for; matrix products, arithmetic and copies ran while one was open for 0% of the time, Pallas kernels for 30%

profile of v3, /device:TPU:25, one launch (start us, length us, event | category | flops | bytes accessed | tf_op | source)
XLA Modules:
  0.0 128.0 jit_solution(4402076676223284039)
XLA Ops:
  0.0 2.1 %shard_map.64 = (f32[256,128]{1,0:T(8,128)}, f32[256,128]{1,0:T(8,128)}) custom-call(bf16[1024,512]{1,0:T(8,128)(2,1)} %record.3), custom_call_target="tpu_custom_call" | custom-call | tf_op jit(solution)/shard_map/pallas_call | solution.py:390
  2.1 3.7 %collective-permute-start.1 = (f32[256,128]{1,0:T(8,128)}, f32[256,128]{1,0:T(8,128)S(1)}, u32[]{:S(2)}, u32[]{:S(2)}) collective-permute-start(f32[256,128]{1,0:T(8,128)} %get-tuple-element.17), channel_id=1, source_target_pairs={{0,1},{1,2},{2,3},{4,5},{5,6},{6,7},{8,9},{9,10},{10,11},{12,13},{... | collective-permute-start | bytes 393224 | tf_op jit(solution)/shard_map/ppermute | solution.py:29
  5.7 1.9 %collective-permute-start.2 = (f32[256,128]{1,0:T(8,128)}, f32[256,128]{1,0:T(8,128)S(1)}, u32[]{:S(2)}, u32[]{:S(2)}) collective-permute-start(f32[256,128]{1,0:T(8,128)} %get-tuple-element.18), channel_id=1, source_target_pairs={{1,0},{2,1},{3,2},{5,4},{6,5},{7,6},{9,8},{10,9},{11,10},{13,12},{... | collective-permute-start | bytes 393224 | tf_op jit(solution)/shard_map/ppermute | solution.py:29
  9.0 3.3 %collective-permute-done.2.right = f32[256,128]{1,0:T(8,128)S(1)} collective-permute-done((f32[256,128]{1,0:T(8,128)}, f32[256,128]{1,0:T(8,128)S(1)}, u32[]{:S(2)}, u32[]{:S(2)}) %collective-permute-start.2) | collective-permute-done | bytes 131104 | tf_op jit(solution)/shard_map/ppermute | solution.py:29
  12.9 2.8 %shard_map.65 = (f32[16,768]{1,0:T(8,128)}, f32[24,768]{1,0:T(8,128)}, f32[248,512]{1,0:T(8,128)}, f32[304,512]{1,0:T(8,128)}, f32[304,512]{1,0:T(8,128)}, /*index=5*/f32[304,512]{1,0:T(8,128)}) custom-call(s32[1]{0:T(128)S(6)} %copy.19.offsets, s32[1]{0:T(128)S(6)} %copy.20.lengths, bf16[1024,512]{1,0:T(8,128)(2,1)} %record.3, f32[256,128]{1,0:T(8,128)} %copy-done.10, ...), custom_call_target="tpu_custom_call" | custom-call | tf_op jit(solution)/shard_map/pallas_call | solution.py:406
  15.7 2.1 %collective-permute-start.4 = (f32[248,512]{1,0:T(8,128)}, f32[248,512]{1,0:T(8,128)S(1)}, u32[]{:S(2)}, u32[]{:S(2)}) collective-permute-start(f32[248,512]{1,0:T(8,128)} %get-tuple-element.20.own.refs_2_), channel_id=1, source_target_pairs={{8,0},{12,4},{16,8},{20,12},{24,16},{28,20},{9,1},{13,5},{17,9},{2... | collective-permute-start | bytes 1523720 | tf_op jit(solution)/shard_map/ppermute | solution.py:29
  17.8 3.1 %collective-permute-start.3 = (f32[24,768]{1,0:T(8,128)}, f32[24,768]{1,0:T(8,128)S(1)}, u32[]{:S(2)}, u32[]{:S(2)}) collective-permute-start(f32[24,768]{1,0:T(8,128)} %get-tuple-element.19), channel_id=1, source_target_pairs={{0,4},{4,8},{8,12},{12,16},{16,20},{20,24},{24,28},{1,5},{5,9},{9,... | collective-permute-start | bytes 221192 | tf_op jit(solution)/shard_map/ppermute | solution.py:29
  20.9 3.1 %collective-permute-done.3.last.refs_1_.refs_6_ = f32[24,768]{1,0:T(8,128)S(1)} collective-permute-done((f32[24,768]{1,0:T(8,128)}, f32[24,768]{1,0:T(8,128)S(1)}, u32[]{:S(2)}, u32[]{:S(2)}) %collective-permute-start.3) | collective-permute-done | bytes 73760 | tf_op jit(solution)/shard_map/ppermute | solution.py:29
  24.6 2.1 %collective-permute-start.6 = (f32[304,512]{1,0:T(8,128)}, f32[304,512]{1,0:T(8,128)S(1)}, u32[]{:S(2)}, u32[]{:S(2)}) collective-permute-start(f32[304,512]{1,0:T(8,128)} %shard_map.68.own.refs_3_), channel_id=1, source_target_pairs={{8,0},{12,4},{16,8},{20,12},{24,16},{28,20},{9,1},{13,5},{17,9},{2... | collective-permute-start | bytes 1867784 | tf_op jit(solution)/shard_map/ppermute | solution.py:29
  27.3 0.8 copy-done
  28.1 1.8 %shard_map.66 = (f32[248,512]{1,0:T(8,128)}, f32[304,512]{1,0:T(8,128)}) custom-call(f32[248,512]{1,0:T(8,128)} %get-tuple-element.20.own.refs_2_, f32[248,512]{1,0:T(8,128)} %copy-done, f32[304,512]{1,0:T(8,128)} %get-tuple-element.21.refs_0_), custom_call_target="tpu_custom_call", output_to_operand_aliasing={{1}: (2, {})} | custom-call | tf_op jit(solution)/shard_map/pallas_call | solution.py:423
  30.0 2.2 %collective-permute-start.5 = (f32[248,512]{1,0:T(8,128)}, f32[248,512]{1,0:T(8,128)S(1)}, u32[]{:S(2)}, u32[]{:S(2)}) collective-permute-start(f32[248,512]{1,0:T(8,128)} %get-tuple-element.22), channel_id=1, source_target_pairs={{0,4},{4,0},{8,12},{12,8},{16,20},{20,16},{24,28},{28,24},{1,5},{5... | collective-permute-start | bytes 1523720 | tf_op jit(solution)/shard_map/ppermute | solution.py:431
  32.2 3.6 %collective-permute-start.7 = (f32[16,768]{1,0:T(8,128)}, f32[16,768]{1,0:T(8,128)S(1)}, u32[]{:S(2)}, u32[]{:S(2)}) collective-permute-start(f32[16,768]{1,0:T(8,128)} %get-tuple-element.25), channel_id=1, source_target_pairs={{12,0},{16,4},{20,8},{24,12},{28,16},{13,1},{17,5},{21,9},{25,13},... | collective-permute-start | bytes 147464 | tf_op jit(solution)/shard_map/ppermute | solution.py:29
  35.9 1.3 %collective-permute-start = (f32[2]{0:T(128)S(1)}, f32[2]{0:T(128)S(1)}, u32[]{:S(2)}, u32[]{:S(2)}) collective-permute-start(f32[2]{0:T(128)S(1)} %add_convert_fusion.mine), channel_id=1, source_target_pairs={{0,8},{4,12},{8,16},{12,20},{16,24},{20,28},{1,9},{5,13},{9,17},{1... | collective-permute-start | bytes 32 | tf_op jit(solution)/shard_map/ppermute | solution.py:29
  37.2 4.0 %collective-permute-start.9 = (f32[304,512]{1,0:T(8,128)}, f32[304,512]{1,0:T(8,128)S(1)}, u32[]{:S(2)}, u32[]{:S(2)}) collective-permute-start(f32[304,512]{1,0:T(8,128)} %get-tuple-element.28.refs_4_.own), channel_id=1, source_target_pairs={{8,0},{12,4},{16,8},{20,12},{24,16},{28,20},{9,1},{13,5},{17,9},{2... | collective-permute-start | bytes 1867784 | tf_op jit(solution)/shard_map/ppermute | solution.py:29
  42.9 1.9 %shard_map.69 = (f32[304,512]{1,0:T(8,128)}, f32[304,512]{1,0:T(8,128)}) custom-call(f32[304,512]{1,0:T(8,128)} %shard_map.68.own.refs_3_, f32[304,512]{1,0:T(8,128)} %copy-done.1, f32[304,512]{1,0:T(8,128)} %get-tuple-element.24.refs_0_, f32[248,512]{1,0:T(8,128)} %copy-done.2, f32[2]{0:T(128)} %copy-done.12, ...), custom_call_target="tpu_custom_call", output_to_operand_aliasing={{1}: (2, {})} | custom-call | tf_op jit(solution)/shard_map/pallas_call | solution.py:423
  44.9 1.9 %collective-permute-start.8 = (f32[304,512]{1,0:T(8,128)}, f32[304,512]{1,0:T(8,128)S(1)}, u32[]{:S(2)}, u32[]{:S(2)}) collective-permute-start(f32[304,512]{1,0:T(8,128)} %get-tuple-element.27), channel_id=1, source_target_pairs={{0,4},{4,0},{8,12},{12,8},{16,20},{20,16},{24,28},{28,24},{1,5},{5... | collective-permute-start | bytes 1867784 | tf_op jit(solution)/shard_map/ppermute | solution.py:431
  46.8 3.5 %collective-permute-start.11 = (f32[304,512]{1,0:T(8,128)}, f32[304,512]{1,0:T(8,128)S(1)}, u32[]{:S(2)}, u32[]{:S(2)}) collective-permute-start(f32[304,512]{1,0:T(8,128)} %get-tuple-element.26.refs_5_.own.refs_3_), channel_id=1, source_target_pairs={{8,0},{12,4},{16,8},{20,12},{24,16},{28,20},{9,1},{13,5},{17,9},{2... | collective-permute-start | bytes 1867784 | tf_op jit(solution)/shard_map/ppermute | solution.py:29
  50.3 1.4 %shard_map.67.params = s32[8,128]{1,0:T(8,128)} custom-call(f32[2]{0:T(128)} %copy-done.12, f32[24,768]{1,0:T(8,128)} %copy-done.7, f32[2]{0:T(128)} %copy-done.13, f32[248,512]{1,0:T(8,128)} %copy-done.2, f32[248,512]{1,0:T(8,128)} %copy-done), custom_call_target="tpu_custom_call" | custom-call | tf_op jit(solution)/shard_map/pallas_call | solution.py:442
  51.7 14.9 %shard_map.70.refs_0_.refs_9_ = f32[1,2048,512]{2,1,0:T(8,128)} custom-call(s32[8,128]{1,0:T(8,128)} %shard_map.67.params, f32[3]{0:T(128)} %thr.7, bf16[768,640]{1,0:T(8,128)(2,1)} %constant.4.clone.refs_0_, bf16[640,512]{1,0:T(8,128)(2,1)} %constant.5.clone.refs_1_, f32[248,512]{1,0:T(8,128)} %get-tuple-element.20.own.refs_2_, ...), custom_call_target="tpu_custom_call" | custom-call | tf_op jit(solution)/shard_map/pallas_call | solution.py:455
  66.6 0.8 copy-done.4
  67.5 0.9 copy-done.3
  68.3 1.9 %shard_map.71 = f32[304,512]{1,0:T(8,128)} custom-call(f32[304,512]{1,0:T(8,128)} %get-tuple-element.28.refs_4_.own, f32[304,512]{1,0:T(8,128)} %copy-done.4, f32[1,2048,512]{2,1,0:T(8,128)} %shard_map.70.refs_0_.refs_9_, f32[304,512]{1,0:T(8,128)} %copy-done.3), custom_call_target="tpu_custom_call" | custom-call | tf_op jit(solution)/shard_map/pallas_call | solution.py:423
  70.3 1.9 %collective-permute-start.10 = (f32[304,512]{1,0:T(8,128)}, f32[304,512]{1,0:T(8,128)S(1)}, u32[]{:S(2)}, u32[]{:S(2)}) collective-permute-start(f32[304,512]{1,0:T(8,128)} %shard_map.71), channel_id=1, source_target_pairs={{0,4},{4,0},{8,12},{12,8},{16,20},{20,16},{24,28},{28,24},{1,5},{5... | collective-permute-start | bytes 1867784 | tf_op jit(solution)/shard_map/ppermute | solution.py:431
  72.1 14.8 %shard_map.72.refs_0_.refs_7_ = f32[1,2048,512]{2,1,0:T(8,128)} custom-call(s32[8,128]{1,0:T(8,128)} %shard_map.67.params, f32[3]{0:T(128)} %thr.7, bf16[768,640]{1,0:T(8,128)(2,1)} %constant.4.clone.refs_0_, bf16[640,512]{1,0:T(8,128)(2,1)} %constant.5.clone.refs_1_, f32[248,512]{1,0:T(8,128)} %get-tuple-element.20.own.refs_2_, ...), custom_call_target="tpu_custom_call", output_to_operand_aliasing={{}: (11, {})} | custom-call | tf_op jit(solution)/shard_map/pallas_call | solution.py:455
  87.0 0.8 copy-done.5
  87.8 0.8 copy-done.6
  88.6 1.9 %shard_map.73 = f32[304,512]{1,0:T(8,128)} custom-call(f32[304,512]{1,0:T(8,128)} %get-tuple-element.26.refs_5_.own.refs_3_, f32[304,512]{1,0:T(8,128)} %copy-done.5, f32[1,2048,512]{2,1,0:T(8,128)} %shard_map.72.refs_0_.refs_7_, f32[304,512]{1,0:T(8,128)} %copy-done.6), custom_call_target="tpu_custom_call" | custom-call | tf_op jit(solution)/shard_map/pallas_call | solution.py:423
  91.0 1.2 shard_map.74.refs_10_
  92.2 13.8 %collective-permute-done.12.refs_7_ = f32[304,512]{1,0:T(8,128)S(1)} collective-permute-done((f32[304,512]{1,0:T(8,128)}, f32[304,512]{1,0:T(8,128)S(1)}, u32[]{:S(2)}, u32[]{:S(2)}) %collective-permute-start.12) | collective-permute-done | bytes 622624 | tf_op jit(solution)/shard_map/ppermute | solution.py:431
  106.0 0.8 copy-done.8
  106.8 21.2 %shard_map.75 = f32[1,2048,512]{2,1,0:T(8,128)} custom-call(s32[8,128]{1,0:T(8,128)} %shard_map.67.params, f32[3]{0:T(128)} %thr.7, bf16[768,640]{1,0:T(8,128)(2,1)} %constant.4.clone.refs_0_, bf16[640,512]{1,0:T(8,128)(2,1)} %constant.5.clone.refs_1_, f32[248,512]{1,0:T(8,128)} %get-tuple-element.20.own.refs_2_, ...), custom_call_target="tpu_custom_call", output_to_operand_aliasing={{}: (12, {})} | custom-call | tf_op jit(solution)/shard_map/pallas_call | solution.py:455
  (35 shorter events, 4.2 us)
Async XLA Ops:
  2.1 6.9 %collective-permute-start.1 = (f32[256,128]{1,0:T(8,128)}, f32[256,128]{1,0:T(8,128)S(1)}, u32[]{:S(2)}, u32[]{:S(2)}) collective-permute-start(f32[256,128]{1,0:T(8,128)} %get-tuple-element.17), channel_id=1, source_target_pairs={{0,1},{1,2},{2,3},{4,5},{5,6},{6,7},{8,9},{9,10},{10,11},{12,13},{... | collective-permute-start | bytes 393224 | tf_op jit(solution)/shard_map/ppermute | solution.py:29
  5.7 6.5 %collective-permute-start.2 = (f32[256,128]{1,0:T(8,128)}, f32[256,128]{1,0:T(8,128)S(1)}, u32[]{:S(2)}, u32[]{:S(2)}) collective-permute-start(f32[256,128]{1,0:T(8,128)} %get-tuple-element.18), channel_id=1, source_target_pairs={{1,0},{2,1},{3,2},{5,4},{6,5},{7,6},{9,8},{10,9},{11,10},{13,12},{... | collective-permute-start | bytes 393224 | tf_op jit(solution)/shard_map/ppermute | solution.py:29
  9.0 3.3 %copy-start.10 = (f32[256,128]{1,0:T(8,128)}, f32[256,128]{1,0:T(8,128)S(1)}, u32[]{:S(2)}) copy-start(f32[256,128]{1,0:T(8,128)S(1)} %collective-permute-done.1.left) | copy-start | bytes 393220
  12.2 0.7 copy-start.11
  15.7 11.7 %collective-permute-start.4 = (f32[248,512]{1,0:T(8,128)}, f32[248,512]{1,0:T(8,128)S(1)}, u32[]{:S(2)}, u32[]{:S(2)}) collective-permute-start(f32[248,512]{1,0:T(8,128)} %get-tuple-element.20.own.refs_2_), channel_id=1, source_target_pairs={{8,0},{12,4},{16,8},{20,12},{24,16},{28,20},{9,1},{13,5},{17,9},{2... | collective-permute-start | bytes 1523720 | tf_op jit(solution)/shard_map/ppermute | solution.py:29
  17.8 6.2 %collective-permute-start.3 = (f32[24,768]{1,0:T(8,128)}, f32[24,768]{1,0:T(8,128)S(1)}, u32[]{:S(2)}, u32[]{:S(2)}) collective-permute-start(f32[24,768]{1,0:T(8,128)} %get-tuple-element.19), channel_id=1, source_target_pairs={{0,4},{4,8},{8,12},{12,16},{16,20},{20,24},{24,28},{1,5},{5,9},{9,... | collective-permute-start | bytes 221192 | tf_op jit(solution)/shard_map/ppermute | solution.py:29
  24.0 0.6 copy-start.7
  24.6 17.3 %collective-permute-start.6 = (f32[304,512]{1,0:T(8,128)}, f32[304,512]{1,0:T(8,128)S(1)}, u32[]{:S(2)}, u32[]{:S(2)}) collective-permute-start(f32[304,512]{1,0:T(8,128)} %shard_map.68.own.refs_3_), channel_id=1, source_target_pairs={{8,0},{12,4},{16,8},{20,12},{24,16},{28,20},{9,1},{13,5},{17,9},{2... | collective-permute-start | bytes 1867784 | tf_op jit(solution)/shard_map/ppermute | solution.py:29
  27.3 0.8 copy-start
  30.0 12.1 %collective-permute-start.5 = (f32[248,512]{1,0:T(8,128)}, f32[248,512]{1,0:T(8,128)S(1)}, u32[]{:S(2)}, u32[]{:S(2)}) collective-permute-start(f32[248,512]{1,0:T(8,128)} %get-tuple-element.22), channel_id=1, source_target_pairs={{0,4},{4,0},{8,12},{12,8},{16,20},{20,16},{24,28},{28,24},{1,5},{5... | collective-permute-start | bytes 1523720 | tf_op jit(solution)/shard_map/ppermute | solution.py:431
  32.2 9.7 %collective-permute-start.7 = (f32[16,768]{1,0:T(8,128)}, f32[16,768]{1,0:T(8,128)S(1)}, u32[]{:S(2)}, u32[]{:S(2)}) collective-permute-start(f32[16,768]{1,0:T(8,128)} %get-tuple-element.25), channel_id=1, source_target_pairs={{12,0},{16,4},{20,8},{24,12},{28,16},{13,1},{17,5},{21,9},{25,13},... | collective-permute-start | bytes 147464 | tf_op jit(solution)/shard_map/ppermute | solution.py:29
  35.9 14.4 %copy-start.13 = (f32[2]{0:T(128)}, f32[2]{0:T(128)S(1)}, u32[]{:S(2)}) copy-start(f32[2]{0:T(128)S(1)} %add_convert_fusion.mine) | copy-start | bytes 28
  35.9 5.3 %collective-permute-start = (f32[2]{0:T(128)S(1)}, f32[2]{0:T(128)S(1)}, u32[]{:S(2)}, u32[]{:S(2)}) collective-permute-start(f32[2]{0:T(128)S(1)} %add_convert_fusion.mine), channel_id=1, source_target_pairs={{0,8},{4,12},{8,16},{12,20},{16,24},{20,28},{1,9},{5,13},{9,17},{1... | collective-permute-start | bytes 32 | tf_op jit(solution)/shard_map/ppermute | solution.py:29
  37.2 29.4 %collective-permute-start.9 = (f32[304,512]{1,0:T(8,128)}, f32[304,512]{1,0:T(8,128)S(1)}, u32[]{:S(2)}, u32[]{:S(2)}) collective-permute-start(f32[304,512]{1,0:T(8,128)} %get-tuple-element.28.refs_4_.own), channel_id=1, source_target_pairs={{8,0},{12,4},{16,8},{20,12},{24,16},{28,20},{9,1},{13,5},{17,9},{2... | collective-permute-start | bytes 1867784 | tf_op jit(solution)/shard_map/ppermute | solution.py:29
  41.2 0.8 copy-start.12
  41.9 0.6 copy-start.9
  41.9 0.8 copy-start.1
  42.1 0.9 copy-start.2
  44.9 21.7 %collective-permute-start.8 = (f32[304,512]{1,0:T(8,128)}, f32[304,512]{1,0:T(8,128)S(1)}, u32[]{:S(2)}, u32[]{:S(2)}) collective-permute-start(f32[304,512]{1,0:T(8,128)} %get-tuple-element.27), channel_id=1, source_target_pairs={{0,4},{4,0},{8,12},{12,8},{16,20},{20,16},{24,28},{28,24},{1,5},{5... | collective-permute-start | bytes 1867784 | tf_op jit(solution)/shard_map/ppermute | solution.py:431
  46.8 40.2 %collective-permute-start.11 = (f32[304,512]{1,0:T(8,128)}, f32[304,512]{1,0:T(8,128)S(1)}, u32[]{:S(2)}, u32[]{:S(2)}) collective-permute-start(f32[304,512]{1,0:T(8,128)} %get-tuple-element.26.refs_5_.own.refs_3_), channel_id=1, source_target_pairs={{8,0},{12,4},{16,8},{20,12},{24,16},{28,20},{9,1},{13,5},{17,9},{2... | collective-permute-start | bytes 1867784 | tf_op jit(solution)/shard_map/ppermute | solution.py:29
  66.6 0.8 copy-start.4
  67.5 0.9 copy-start.3
  70.3 16.7 %collective-permute-start.10 = (f32[304,512]{1,0:T(8,128)}, f32[304,512]{1,0:T(8,128)S(1)}, u32[]{:S(2)}, u32[]{:S(2)}) collective-permute-start(f32[304,512]{1,0:T(8,128)} %shard_map.71), channel_id=1, source_target_pairs={{0,4},{4,0},{8,12},{12,8},{16,20},{20,16},{24,28},{28,24},{1,5},{5... | collective-permute-start | bytes 1867784 | tf_op jit(solution)/shard_map/ppermute | solution.py:431
  87.0 0.8 copy-start.5
  87.8 0.8 copy-start.6
  90.6 15.4 %collective-permute-start.12 = (f32[304,512]{1,0:T(8,128)}, f32[304,512]{1,0:T(8,128)S(1)}, u32[]{:S(2)}, u32[]{:S(2)}) collective-permute-start(f32[304,512]{1,0:T(8,128)} %shard_map.73), channel_id=1, source_target_pairs={{0,4},{4,0},{8,12},{12,8},{16,20},{20,16},{24,28},{28,24},{1,5},{5... | collective-permute-start | bytes 1867784 | tf_op jit(solution)/shard_map/ppermute | solution.py:431
  106.0 0.8 copy-start.8
